TPU v7x, 128 devices: a whole 4x4x4 slice. The times are simulated.
128 devices in a mesh: dp: 16 (over x, z), tensor: 8 (over y, core).
Axes of the slice: x: 4, y: 4, z: 4, core: 2. Of those that a mesh axis runs over, the one named last changes fastest.
Arguments:
- normed_input: bfloat16 [16384, 6144], P('dp'), may hold values from -120 to 120
- query_grad: bfloat16 [16384, 6144], P('dp', 'tensor'), may hold values from -45 to 45
- query_weight: bfloat16 [6144, 6144], P('dp', 'tensor'), may hold values from -0.078125 to 0.078125
Outputs:
- input_grad: bfloat16 [16384, 6144], P('dp', 'tensor')
- weight_grad: float32 [6144, 6144], P('dp', 'tensor')
- grad_peak: float32 [], replicated
All inputs are finite; a program needn't handle non-finite values.
Results may differ from a plain program's by a relative error of at most 0.02.
Values may be sent and summed in bfloat16 or wider, within the bound.
No kernel may reach another device: no remote copies, remote signals or barrier semaphores. Data moves between devices by JAX's collectives and lax.ppermute only.
A program may use at most 192 MiB of HBM per device.

v0:
```python
import jax
import jax.numpy as jnp
from jax import lax
from jax.sharding import PartitionSpec as P


def per_device(normed_input, query_grad, query_weight):
    replica_grad = jnp.dot(normed_input.T, query_grad, preferred_element_type=jnp.float32)
    local_peak = jnp.max(jnp.abs(replica_grad))
    grad_peak = lax.pmax(local_peak, ("dp", "tensor"))
    weight_grad = lax.psum_scatter(
        (replica_grad / grad_peak).astype(jnp.bfloat16), "dp", scatter_dimension=0, tiled=True
    ).astype(jnp.float32)
    partial_value = jnp.dot(
        query_grad,
        lax.all_gather(query_weight, "dp", axis=0, tiled=True).T,
        preferred_element_type=jnp.float32,
    )
    block_part = partial_value.astype(jnp.bfloat16)
    summed = lax.psum_scatter(
        block_part.astype(jnp.float32).astype(jnp.bfloat16),
        "tensor",
        scatter_dimension=1,
        tiled=True,
    )
    return (summed, weight_grad, grad_peak)


def solution(mesh):
    return jax.shard_map(
        per_device,
        mesh=mesh,
        in_specs=(P("dp", None), P("dp", "tensor"), P("dp", "tensor")),
        out_specs=(P("dp", "tensor"), P("dp", "tensor"), P()),
        check_vma=False,
    )
```

profile of v0, /device:TPU:0, one launch (start us, length us, event | category | flops | bytes accessed | tf_op | source)
XLA Modules:
  0.0 272.9 jit_solution(6729459180537028647)
XLA Ops:
  7.2 0.0 copy-start
  7.2 0.0 all-gather.2.cloned.1.call-start
  7.2 0.7 all-gather.2.cloned.1.call-update
  7.9 0.0 reduce-scatter.5.cloned.1.call-start
  8.0 0.6 copy-done
  8.6 17.7 %abs_reduce_fusion = (f32[]{:T(128)}, f32[6144,768]{1,0:T(8,128)}) fusion(bf16[1024,6144]{1,0:T(8,128)(2,1)} %param.3, bf16[1024,768]{1,0:T(8,128)(2,1)S(1)} %copy-done), kind=kOutput, calls=%fused_computation.1 | convolution fusion | flops 9673113600 | bytes 33030148 | tf_op jit(solution)/shard_map/dot_general | solution.py:8
  26.2 69.5 %pmax.7 = f32[]{:T(128)} all-reduce(f32[]{:T(128)} %get-tuple-element.3), channel_id=1, replica_groups=mesh['dp'=16,'tensor'=8] {'dp','tensor'}, use_global_device_ids=true, to_apply=%region_2.0 | all-reduce | flops 1 | bytes 8 | tf_op jit(solution)/shard_map/pmax | solution.py:10
  95.7 12.1 %divide_convert_fusion = bf16[6144,768]{1,0:T(8,128)(2,1)} fusion(f32[6144,768]{1,0:T(8,128)} %get-tuple-element.4, f32[]{:T(128)} %pmax.7), kind=kLoop, calls=%fused_computation | loop fusion | flops 9437184 | bytes 28311556 | tf_op jit(solution)/shard_map/convert_element_type | solution.py:12
  107.8 0.0 reduce-scatter.5.cloned.1.call-update
  107.8 0.0 reduce-scatter.3.cloned.1.call-start
  107.9 0.0 all-gather.2.cloned.1.call-done
  107.9 16.2 %convolution_convert_fusion = bf16[1024,6144]{1,0:T(8,128)(2,1)} fusion(bf16[1024,768]{1,0:T(8,128)(2,1)S(1)} %copy-done, bf16[6144,768]{1,0:T(8,128)(2,1)} %all-gather.2.cloned.1.call-done), kind=kOutput, calls=%fused_computation.2 | convolution fusion | flops 9669967872 | bytes 23592960 | tf_op jit(solution)/shard_map/dot_general | solution.py:14
  124.1 0.0 reduce-scatter.3.cloned.1.call-update
  124.1 67.6 %reduce-scatter.5.cloned.1.call-done = bf16[384,768]{1,0:T(8,128)(2,1)} async-done(((bf16[6144,768]{1,0:T(8,128)(2,1)}), bf16[384,768]{1,0:T(8,128)(2,1)}) %reduce-scatter.5.cloned.1.call-update) | async-done | bytes 589840 | tf_op jit(solution)/shard_map/reduce_scatter | solution.py:11
  191.7 2.2 convert_element_type.13
  193.8 72.5 %reduce-scatter.3.cloned.1.call-done = bf16[1024,768]{1,0:T(8,128)(2,1)} async-done(((bf16[1024,6144]{1,0:T(8,128)(2,1)}), bf16[1024,768]{1,0:T(8,128)(2,1)}) %reduce-scatter.3.cloned.1.call-update) | async-done | bytes 1572880 | tf_op jit(solution)/shard_map/reduce_scatter | solution.py:20
Async XLA Ops:
  7.2 1.4 copy-start
  7.2 100.7 %all-gather.2.cloned.1.call-start = ((), (), s32[]{:S(2)}) async-start(), calls=%async_computation.2 | async-start | bytes 10027008 | tf_op jit(solution)/shard_map/all_gather | solution.py:16
  7.9 183.8 %reduce-scatter.5.cloned.1.call-start = ((), (), s32[]{:S(2)}) async-start(), calls=%async_computation.4 | async-start | bytes 10027008 | tf_op jit(solution)/shard_map/reduce_scatter | solution.py:11
  107.8 158.5 %reduce-scatter.3.cloned.1.call-start = ((), (), s32[]{:S(2)}) async-start(), calls=%async_computation.3 | async-start | bytes 14155776 | tf_op jit(solution)/shard_map/reduce_scatter | solution.py:20
Sparse Core Ops, SparseCore 0:
  10.2 79.2 all-gather.1
  108.0 83.6 reduce-scatter.4
  194.8 71.4 reduce-scatter.2
where the time goes:
time: 273 us
  waiting for transfers between devices  141 us (52%)
  blocking collectives  69.5 us (25%)
  matrix products  33.8 us (12%)
  other arithmetic  14.3 us (5%)
  between operations  13.8 us (5%)
    reduce_scatter x1, waiting for transfers between devices, per_device(): lax.psum_scatter(block_part.astype(jnp.float32).astype(jnp.bfloat16), 'te...  72.5 us
    pmax x1, blocking collectives, per_device(): grad_peak = lax.pmax(local_peak, ('dp', 'tensor'))  69.5 us
    reduce_scatter x1, waiting for transfers between devices, per_device(): lax.psum_scatter((replica_grad / grad_peak).astype(jnp.bfloat16), 'dp', s...  67.6 us
    dot_general x1, matrix products, per_device(): jnp.dot(normed_input.T, query_grad, preferred_element_type=jnp.float32)  17.7 us
    dot_general x1, matrix products, per_device(): jnp.dot(query_grad, lax.all_gather(query_weight, 'dp', axis=0, tiled=True...  16.2 us
    convert_element_type x1, other arithmetic, per_device(): (replica_grad / grad_peak).astype(jnp.bfloat16)  12.1 us
  transfers between devices with their start and end apart: 3, of which 2 were waited for; matrix products, arithmetic and copies ran while one was open for 18% of the time, Pallas kernels for 0%

commit v1 on v0

v1 whole, which is shorter than its diff:
```python
import jax
import jax.numpy as jnp
import numpy as np
from jax import lax
from jax.experimental import pallas as pl
from jax.experimental.pallas import tpu as pltpu
from jax.sharding import PartitionSpec as P

F32, BF16 = jnp.float32, jnp.bfloat16
AXES = ("dp", "tensor")
NX, NY, NZ = 4, 4, 4
CHUNKS = 2


def permutation(move):
    pairs = []
    for x in range(NX):
        for z in range(NZ):
            for y in range(NY):
                for c in range(2):
                    to = move(x, y, z, c)
                    pairs.append((flat(x, y, z, c), flat(*to)))
    return pairs


def flat(x, y, z, c):
    return ((x % NX) * NZ + z % NZ) * NY * 2 + (y % NY) * 2 + c % 2


def step_along(second, d):
    def move(x, y, z, c):
        return (x + d, y, z, c) if (c ^ second) == 0 else (x, y, z + d, c)

    return permutation(move)


FIRST = {d: step_along(0, d) for d in (1, -1, 2)}
SECOND = {d: step_along(1, d) for d in (1, -1, 2)}
HAND_ON = permutation(lambda x, y, z, c: (x, y + 1 - 2 * c, z, c))
SIBLING = permutation(lambda x, y, z, c: (x, y, z, c + 1))
HALVINGS = (
    SIBLING,
    permutation(lambda x, y, z, c: (x, y + 1, z, c)),
    permutation(lambda x, y, z, c: (x, y + 2, z, c)),
    permutation(lambda x, y, z, c: (x + 1, y, z, c)),
    permutation(lambda x, y, z, c: (x + 2, y, z, c)),
    permutation(lambda x, y, z, c: (x, y, z + 1, c)),
    permutation(lambda x, y, z, c: (x, y, z + 2, c)),
)


def send(value, pairs):
    return lax.ppermute(value, AXES, pairs)


def add(*terms):
    total = terms[0].astype(F32)
    for term in terms[1:]:
        total = total + term.astype(F32)
    return total


W_ORDER = (
    [(2, 0), (2, 1), (1, 2), (1, 3)]
    + [(2, 2), (2, 3), (3, 0), (3, 1)]
    + [(1, 0), (1, 1), (3, 2), (3, 3)]
    + [(0, 0), (0, 1), (0, 2), (0, 3)]
)


def weight_kernel(order, x_ref, g_ref, plus_ref, minus_ref, rest_ref, peak_ref, gt_ref):
    n = pl.program_id(0)

    @pl.when(n == 0)
    def _():
        gt_ref[...] = g_ref[...].T
        peak_ref[...] = jnp.zeros_like(peak_ref)

    out = jnp.dot(gt_ref[...], x_ref[...], preferred_element_type=F32)
    rows, cols = out.shape
    peak_ref[...] = jnp.maximum(
        peak_ref[...], jnp.max(jnp.abs(out).reshape(rows // 8, 8, cols), axis=0)
    )
    low = out.astype(BF16)

    @pl.when(n < 4)
    def _():
        plus_ref[0] = low

    @pl.when((n >= 4) & (n < 8))
    def _():
        minus_ref[0] = low

    @pl.when(n >= 8)
    def _():
        rest_ref[0] = low


def weight_products(order, base, x, g):
    tokens, d = x.shape
    cols = g.shape[1]
    rows = d // 16
    grid_spec = pltpu.PrefetchScalarGridSpec(
        num_scalar_prefetch=1,
        grid=(16,),
        in_specs=[
            pl.BlockSpec((tokens, rows), lambda n, o: (0, o[base + n])),
            pl.BlockSpec((tokens, cols), lambda n, o: (0, 0)),
        ],
        out_specs=[
            pl.BlockSpec((1, cols, rows), lambda n, o: (jnp.minimum(n, 3), 0, 0)),
            pl.BlockSpec((1, cols, rows), lambda n, o: (jnp.clip(n - 4, 0, 3), 0, 0)),
            pl.BlockSpec((1, cols, rows), lambda n, o: (jnp.maximum(n - 8, 0), 0, 0)),
            pl.BlockSpec((8, rows), lambda n, o: (0, 0)),
        ],
        scratch_shapes=[pltpu.VMEM((cols, tokens), BF16)],
    )
    return pl.pallas_call(
        weight_kernel,
        grid_spec=grid_spec,
        out_shape=[
            jax.ShapeDtypeStruct((4, cols, rows), BF16),
            jax.ShapeDtypeStruct((4, cols, rows), BF16),
            jax.ShapeDtypeStruct((8, cols, rows), BF16),
            jax.ShapeDtypeStruct((8, rows), F32),
        ],
        compiler_params=pltpu.CompilerParams(vmem_limit_bytes=40 * 2**20),
        cost_estimate=pl.CostEstimate(flops=1, bytes_accessed=1, transcendentals=0),
        name="weight_products",
    )(order, x, g)


def tables():
    rows = []
    for dp in range(NX * NZ):
        for t in range(NY * 2):
            x, z, y, c = dp // NZ, dp % NZ, t // 2, t % 2
            row = []
            for core in (1 - c, c):
                for d in I_DEST:
                    fx = (y + (d if c == 0 else -d)) % NY
                    for e in range(2):
                        fz = 2 * core + e
                        off_x, off_z = (x - fx) % NX, (z - fz) % NZ
                        i, j = (off_x, off_z) if c == 0 else (off_z, off_x)
                        row.append(SLOT[j] * 4 + SLOT[i])
            for first, second in W_ORDER:
                rx, rz = (first, second) if c == 0 else (second, first)
                row.append(((x + rx) % NX) * NZ + (z + rz) % NZ)
            rows.append(row)
    return np.array(rows, np.int32)


SLOT = (0, 1, 3, 2)
I_DEST = (3, 2, 1, 0)
NT = (((1,), (1,)), ((), ()))


def give_kernel(order, g_ref, w0, w1, out_ref):
    w = jnp.concatenate([w0[0], w1[0]], axis=0)
    out_ref[0] = lax.dot_general(g_ref[...], w, NT, preferred_element_type=F32).astype(BF16)


def keep_kernel(order, g_ref, w0, w1, got_ref, first_ref, rest_ref):
    n = pl.program_id(0)
    w = jnp.concatenate([w0[0], w1[0]], axis=0)
    out = lax.dot_general(g_ref[...], w, NT, preferred_element_type=F32)
    low = (out + got_ref[0].astype(F32)).astype(BF16)

    @pl.when(n == 0)
    def _():
        first_ref[0] = low

    @pl.when(n > 0)
    def _():
        rest_ref[0] = low


def input_products(order, base, g, w, got=None):
    tokens, k = g.shape
    rows = w.shape[1]
    shape = (1, tokens, 2 * rows)

    def w_spec(e):
        return pl.BlockSpec((1, rows, k), lambda n, o: (o[base + 2 * n + e], 0, 0))

    in_specs = [pl.BlockSpec((tokens, k), lambda n, o: (0, 0)), w_spec(0), w_spec(1)]
    args = [g, w, w]
    if got is None:
        out_specs = pl.BlockSpec(shape, lambda n, o: (n, 0, 0))
        out_shape = jax.ShapeDtypeStruct((4,) + shape[1:], BF16)
    else:
        in_specs.append(pl.BlockSpec(shape, lambda n, o: (jnp.where(n == 3, 3, 2 - n), 0, 0)))
        args.append(got)
        out_specs = [
            pl.BlockSpec(shape, lambda n, o: (0, 0, 0)),
            pl.BlockSpec(shape, lambda n, o: (jnp.maximum(n - 1, 0), 0, 0)),
        ]
        out_shape = [
            jax.ShapeDtypeStruct(shape, BF16),
            jax.ShapeDtypeStruct((3,) + shape[1:], BF16),
        ]
    return pl.pallas_call(
        give_kernel if got is None else keep_kernel,
        grid_spec=pltpu.PrefetchScalarGridSpec(
            num_scalar_prefetch=1, grid=(4,), in_specs=in_specs, out_specs=out_specs
        ),
        out_shape=out_shape,
        compiler_params=pltpu.CompilerParams(vmem_limit_bytes=40 * 2**20),
        cost_estimate=pl.CostEstimate(flops=1, bytes_accessed=1, transcendentals=0),
        name="give_products" if got is None else "keep_products",
    )(order, *args)


def tie_kernel(*refs):
    pass


def tie(value, *after):
    spec = pl.BlockSpec(memory_space=pl.ANY)
    return pl.pallas_call(
        tie_kernel,
        in_specs=[spec] * (1 + len(after)),
        out_specs=spec,
        out_shape=jax.ShapeDtypeStruct(value.shape, value.dtype),
        input_output_aliases={0: 0},
        cost_estimate=pl.CostEstimate(flops=1, bytes_accessed=1, transcendentals=0),
        name="tie",
    )(value, *after)


def per_device(x_in, g, w):
    dp = lax.axis_index("dp")
    t = lax.axis_index("tensor")
    table = tables()
    order = lax.dynamic_index_in_dim(jnp.asarray(table), dp * NY * 2 + t, 0, keepdims=False)

    near = [w, send(w, FIRST[1]), send(w, FIRST[-1]), send(w, FIRST[2])]
    plus, minus, rest, peak8 = weight_products(order, 16, x_in, g)
    near[3] = tie(near[3], peak8)

    part = w.shape[0] // CHUNKS
    lines = [jnp.stack([b[j * part : (j + 1) * part] for b in near]) for j in range(CHUNKS)]
    wholes = []
    for line in lines:
        up, down = send(line, SECOND[1]), send(line, SECOND[-1])
        far = [send(up[:2], SECOND[1]), send(down[2:], SECOND[-1])]
        wholes.append(jnp.concatenate([line, up, down] + far, axis=0))

    u, v = send(plus, FIRST[1]), send(minus, FIRST[-1])
    r = send(add(rest[0:2], u[0:2]).astype(BF16), FIRST[1])
    s = send(add(rest[2:4], v[0:2]).astype(BF16), FIRST[-1])
    e = [add(rest[4], v[2], r[0]), add(rest[5], v[3], r[1]), add(rest[6], u[2], s[0]), add(rest[7], u[3], s[1])]
    e = [b.astype(BF16) for b in e]
    h = e[0].shape[0] // 2
    u = send(jnp.stack([e[2][:h], e[1][h:]]), SECOND[1])
    v = send(jnp.stack([e[2][h:], e[3][:h]]), SECOND[-1])
    r = send(add(e[1][:h], u[0]).astype(BF16), SECOND[1])
    s = send(add(e[3][h:], v[0]).astype(BF16), SECOND[-1])
    total = jnp.concatenate([add(e[0][:h], v[1], r), add(e[0][h:], u[1], s)], axis=0)

    pieces = []
    for whole in wholes:
        got = send(input_products(order, 0, g, whole), SIBLING)
        first, others = input_products(order, 8, g, whole, got)
        hop = send(first[0], HAND_ON)
        hop = send(add(others[0], hop).astype(BF16), HAND_ON)
        hop = send(add(others[1], hop).astype(BF16), HAND_ON)
        pieces.append(add(others[2], hop).astype(BF16))

    peak = jnp.broadcast_to(jnp.max(peak8), (1, 128))
    for pairs in HALVINGS:
        peak = jnp.maximum(peak, send(peak, pairs))
    grad_peak = peak[0, 0]
    weight_grad = total.T / grad_peak
    input_grad = jnp.concatenate([p[:, e * part : (e + 1) * part] for e in range(2) for p in pieces], axis=1)
    return input_grad, weight_grad, grad_peak


def solution(mesh):
    return jax.shard_map(
        per_device,
        mesh=mesh,
        in_specs=(P("dp", None), P("dp", "tensor"), P("dp", "tensor")),
        out_specs=(P("dp", "tensor"), P("dp", "tensor"), P()),
        check_vma=False,
    )
```

time: 273 us -> 222 us (0.81)
  blocking collectives: 69.5 us -> 0 us
  starting transfers between devices: 0.12 us -> 48.1 us
  waiting for transfers between devices: 141 us -> 95.7 us
  Pallas kernels: 0 us -> 42.9 us
  matrix products: 33.8 us -> 0 us
  local copies, waits for them, and re-layouts: 0.63 us -> 17.1 us
  between operations: 13.8 us -> 1.19 us
    reduce_scatter x2 -> x0, waiting for transfers between devices: 140 us -> none  [the longest x1 72.5 us: per_device(): lax.psum_scatter(block_part.astype(jnp.float32).astype(jnp.bfloat16), 'te...]
    ppermute x0 -> x34, waiting for transfers between devices: none -> 95.7 us  [send(): return lax.ppermute(value, AXES, pairs)]
    pmax x1 -> x0, blocking collectives: 69.5 us -> none  [per_device(): grad_peak = lax.pmax(local_peak, ('dp', 'tensor'))]
    ppermute x0 -> x34, starting transfers between devices: none -> 48.1 us  [send(): return lax.ppermute(value, AXES, pairs)]
    pallas_call x0 -> x6, Pallas kernels: none -> 42.9 us  [the longest x4 23.2 us: input_products(): pl.pallas_call(give_kernel if got is None else keep_kernel, grid_spec=plt...]
    dot_general x2 -> x0, matrix products: 33.8 us -> none  [the longest x1 17.7 us: per_device(): jnp.dot(normed_input.T, query_grad, preferred_element_type=jnp.float32)]
    unnamed x2 -> x53, local copies, waits for them, and re-layouts: 0.63 us -> 12.6 us
    convert_element_type x2 -> x10, other arithmetic: 14.3 us -> 11.8 us  [the longest x1 3.68 us: per_device(): e = [b.astype(BF16) for b in e]]
  transfers between devices with their start and end apart: 3 -> 34, of which waited for: 2 -> 15; matrix products, arithmetic and copies ran while one was open for 18% -> 9% of each run, Pallas kernels for 0% -> 19%
where the time goes in v1:
time: 222 us; the launch traced here: 221 us
  waiting for transfers between devices  95.7 us (43%)
  starting transfers between devices  48.1 us (22%)
  Pallas kernels  42.9 us (19%)
  local copies, waits for them, and re-layouts  17.1 us (8%)
  other arithmetic  16.3 us (7%)
    ppermute x34, waiting for transfers between devices, send(): return lax.ppermute(value, AXES, pairs)  95.7 us
    ppermute x34, starting transfers between devices, send(): return lax.ppermute(value, AXES, pairs)  48.1 us
    pallas_call x4, Pallas kernels, input_products(): pl.pallas_call(give_kernel if got is None else keep_kernel, grid_spec=plt...  23.2 us
    pallas_call x1, Pallas kernels, weight_products(): pl.pallas_call(weight_kernel, grid_spec=grid_spec, out_shape=[jax.ShapeDt...  19.7 us
    unnamed x53, local copies, waits for them, and re-layouts  12.6 us
  transfers between devices with their start and end apart: 34, of which 15 were waited for; matrix products, arithmetic and copies ran while one was open for 9% of the time, Pallas kernels for 19%

profile of v1, /device:TPU:0, one launch (start us, length us, event | category | flops | bytes accessed | tf_op | source)
XLA Modules:
  0.0 221.3 jit_solution(16279770780072967279)
XLA Ops:
  0.6 3.2 %collective-permute-start.2 = (bf16[384,768]{1,0:T(8,128)(2,1)}, bf16[384,768]{1,0:T(8,128)(2,1)S(1)}, u32[]{:S(2)}, u32[]{:S(2)}) collective-permute-start(bf16[384,768]{1,0:T(8,128)(2,1)} %param.6), channel_id=1, source_target_pairs={{0,64},{1,17},{2,66},{3,19},{4,68},{5,21},{6,70},{7,23},{8,72},{9,... | collective-permute-start | bytes 1769480 | tf_op jit(solution)/shard_map/ppermute | solution.py:53
  4.4 2.6 %collective-permute-start.1 = (bf16[384,768]{1,0:T(8,128)(2,1)}, bf16[384,768]{1,0:T(8,128)(2,1)S(1)}, u32[]{:S(2)}, u32[]{:S(2)}) collective-permute-start(bf16[384,768]{1,0:T(8,128)(2,1)} %param.6), channel_id=1, source_target_pairs={{0,96},{1,25},{2,98},{3,27},{4,100},{5,29},{6,102},{7,31},{8,104},... | collective-permute-start | bytes 1769480 | tf_op jit(solution)/shard_map/ppermute | solution.py:53
  8.8 1.4 copy-done.4
  10.3 19.7 %weight_products.1 = (bf16[4,768,384]{2,1,0:T(8,128)(2,1)S(1)}, bf16[4,768,384]{2,1,0:T(8,128)(2,1)S(1)}, bf16[8,768,384]{2,1,0:T(8,128)(2,1)S(1)}, f32[8,384]{1,0:T(8,128)S(1)}) custom-call(s32[32]{0:T(128)S(1)} %dynamic-slice_bitcast_fusion.order, bf16[1024,6144]{1,0:T(8,128)(2,1)} %x_ref.1, bf16[1024,768]{1,0:T(8,128)(2,1)S(1)} %copy-done.4), custom_call_target="tpu_custom_call" | custom-call | flops 1 | bytes 1 | tf_op jit(solution)/shard_map/weight_products/pallas_call | solution.py:118
  29.9 2.2 copy-done.6
  32.7 1.4 copy-done.11
  34.1 1.5 copy-done.13
  37.8 2.0 collective-permute-start.3
  39.8 2.2 collective-permute-start.4
  42.2 3.2 %collective-permute-start.12 = (bf16[4,192,768]{2,1,0:T(8,128)(2,1)S(1)}, bf16[4,192,768]{2,1,0:T(8,128)(2,1)S(1)}, u32[]{:S(2)}, u32[]{:S(2)}) collective-permute-start(bf16[4,192,768]{2,1,0:T(8,128)(2,1)S(1)} %pad_maximum_fusion.2), channel_id=1, source_target_pairs={{0,24},{1,97},{2,26},{3,99},{4,28},{5,101},{6,30},{7,103},{8,0},{9... | collective-permute-start | bytes 3538952 | tf_op jit(solution)/shard_map/ppermute | solution.py:53
  45.6 10.5 %collective-permute-done.3 = bf16[4,192,768]{2,1,0:T(8,128)(2,1)S(1)} collective-permute-done((bf16[4,192,768]{2,1,0:T(8,128)(2,1)S(1)}, bf16[4,192,768]{2,1,0:T(8,128)(2,1)S(1)}, u32[]{:S(2)}, u32[]{:S(2)}) %collective-permute-start.3) | collective-permute-done | bytes 1179680 | tf_op jit(solution)/shard_map/ppermute | solution.py:53
  56.2 11.5 %collective-permute-done.4 = bf16[4,192,768]{2,1,0:T(8,128)(2,1)S(1)} collective-permute-done((bf16[4,192,768]{2,1,0:T(8,128)(2,1)S(1)}, bf16[4,192,768]{2,1,0:T(8,128)(2,1)S(1)}, u32[]{:S(2)}, u32[]{:S(2)}) %collective-permute-start.4) | collective-permute-done | bytes 1179680 | tf_op jit(solution)/shard_map/ppermute | solution.py:53
  67.8 5.4 %collective-permute-done.11 = bf16[4,192,768]{2,1,0:T(8,128)(2,1)S(1)} collective-permute-done((bf16[4,192,768]{2,1,0:T(8,128)(2,1)S(1)}, bf16[4,192,768]{2,1,0:T(8,128)(2,1)S(1)}, u32[]{:S(2)}, u32[]{:S(2)}) %collective-permute-start.11) | collective-permute-done | bytes 1179680 | tf_op jit(solution)/shard_map/ppermute | solution.py:53
  73.2 5.4 %collective-permute-start.6 = (bf16[2,192,768]{2,1,0:T(8,128)(2,1)S(1)}, bf16[2,192,768]{2,1,0:T(8,128)(2,1)S(1)}, u32[]{:S(2)}, u32[]{:S(2)}) collective-permute-start(bf16[2,192,768]{2,1,0:T(8,128)(2,1)S(1)} %slice.228), channel_id=1, source_target_pairs={{0,24},{1,97},{2,26},{3,99},{4,28},{5,101},{6,30},{7,103},{8,0},{9... | collective-permute-start | bytes 1769480 | tf_op jit(solution)/shard_map/ppermute | solution.py:53
  78.8 14.2 %collective-permute-done.12 = bf16[4,192,768]{2,1,0:T(8,128)(2,1)S(1)} collective-permute-done((bf16[4,192,768]{2,1,0:T(8,128)(2,1)S(1)}, bf16[4,192,768]{2,1,0:T(8,128)(2,1)S(1)}, u32[]{:S(2)}, u32[]{:S(2)}) %collective-permute-start.12) | collective-permute-done | bytes 1179680 | tf_op jit(solution)/shard_map/ppermute | solution.py:53
  93.0 2.4 %collective-permute-start.13 = (bf16[2,192,768]{2,1,0:T(8,128)(2,1)S(1)}, bf16[2,192,768]{2,1,0:T(8,128)(2,1)S(1)}, u32[]{:S(2)}, u32[]{:S(2)}) collective-permute-start(bf16[2,192,768]{2,1,0:T(8,128)(2,1)S(1)} %slice.233), channel_id=1, source_target_pairs={{0,8},{1,33},{2,10},{3,35},{4,12},{5,37},{6,14},{7,39},{8,16},{9,4... | collective-permute-start | bytes 1769480 | tf_op jit(solution)/shard_map/ppermute | solution.py:53
  95.6 1.3 collective-permute-start.14
  97.0 3.2 %collective-permute-done.6 = bf16[2,192,768]{2,1,0:T(8,128)(2,1)S(1)} collective-permute-done((bf16[2,192,768]{2,1,0:T(8,128)(2,1)S(1)}, bf16[2,192,768]{2,1,0:T(8,128)(2,1)S(1)}, u32[]{:S(2)}, u32[]{:S(2)}) %collective-permute-start.6) | collective-permute-done | bytes 589856 | tf_op jit(solution)/shard_map/ppermute | solution.py:53
  100.3 5.5 %give_products.2 = bf16[4,1024,384]{2,1,0:T(8,128)(2,1)} custom-call(s32[32]{0:T(128)S(1)} %dynamic-slice_bitcast_fusion.order, bf16[1024,768]{1,0:T(8,128)(2,1)S(1)} %copy-done.5, bf16[16,192,768]{2,1,0:T(8,128)(2,1)S(1)} %constant_dynamic-update-slice_fusion.w0.w1, bf16[16,192,768]{2,1,0:T(8,128)(2,1)S(1)} %constant_dynamic-update-slice_fusion.w0.w1), custom_call_target="tpu_custom_call" | custom-call | flops 1 | bytes 1 | tf_op jit(solution)/shard_map/give_products/pallas_call | solution.py:203
  106.8 5.5 %give_products.3 = bf16[4,1024,384]{2,1,0:T(8,128)(2,1)} custom-call(s32[32]{0:T(128)S(1)} %dynamic-slice_bitcast_fusion.order, bf16[1024,768]{1,0:T(8,128)(2,1)S(1)} %copy-done.5, bf16[16,192,768]{2,1,0:T(8,128)(2,1)S(1)} %constant_dynamic-update-slice_fusion.8.w0.w1, bf16[16,192,768]{2,1,0:T(8,128)(2,1)S(1)} %constant_dynamic-update-slice_fusion.8.w0.w1), custom_call_target="tpu_custom_call" | custom-call | flops 1 | bytes 1 | tf_op jit(solution)/shard_map/give_products/pallas_call | solution.py:203
  112.3 3.6 %add_convert_fusion.1 = (bf16[2,768,384]{2,1,0:T(8,128)(2,1)}, bf16[2,768,384]{2,1,0:T(8,128)(2,1)}) fusion(bf16[4,768,384]{2,1,0:T(8,128)(2,1)} %collective-permute-done.20, bf16[8,768,384]{2,1,0:T(8,128)(2,1)S(1)} %bitcast.67, bf16[4,768,384]{2,1,0:T(8,128)(2,1)} %collective-permute-done.19), kind=kLoop, calls=%fused_computation.1 | loop fusion | flops 4718592 | bytes 7077888 | tf_op jit(solution)/shard_map/convert_element_type | solution.py:251
  115.9 3.2 %collective-permute-start.22 = (bf16[2,768,384]{2,1,0:T(8,128)(2,1)}, bf16[2,768,384]{2,1,0:T(8,128)(2,1)}, u32[]{:S(2)}, u32[]{:S(2)}) collective-permute-start(bf16[2,768,384]{2,1,0:T(8,128)(2,1)} %get-tuple-element.29), channel_id=1, source_target_pairs={{0,96},{1,25},{2,98},{3,27},{4,100},{5,29},{6,102},{7,31},{8,104},... | collective-permute-start | bytes 3538952 | tf_op jit(solution)/shard_map/ppermute | solution.py:53
  120.9 2.3 %copy-done.1 = bf16[16,192,768]{2,1,0:T(8,128)(2,1)S(1)} copy-done((bf16[16,192,768]{2,1,0:T(8,128)(2,1)S(1)}, bf16[16,192,768]{2,1,0:T(8,128)(2,1)}, u32[]{:S(2)}) %copy-start.1) | copy-done | bytes 4718616
  123.2 6.1 %keep_products.2 = (bf16[1,1024,384]{2,1,0:T(8,128)(2,1)S(1)}, bf16[3,1024,384]{2,1,0:T(8,128)(2,1)S(1)}) custom-call(s32[32]{0:T(128)S(1)} %dynamic-slice_bitcast_fusion.order, bf16[1024,768]{1,0:T(8,128)(2,1)S(1)} %copy-done.5, bf16[16,192,768]{2,1,0:T(8,128)(2,1)S(1)} %copy-done.1, bf16[16,192,768]{2,1,0:T(8,128)(2,1)S(1)} %copy-done.1, ...), custom_call_target="tpu_custom_call" | custom-call | flops 1 | bytes 1 | tf_op jit(solution)/shard_map/keep_products/pallas_call | solution.py:203
  129.4 1.6 collective-permute-start.8
  131.0 2.5 %collective-permute-done.21 = bf16[2,768,384]{2,1,0:T(8,128)(2,1)S(1)} collective-permute-done((bf16[2,768,384]{2,1,0:T(8,128)(2,1)}, bf16[2,768,384]{2,1,0:T(8,128)(2,1)S(1)}, u32[]{:S(2)}, u32[]{:S(2)}) %collective-permute-start.21) | collective-permute-done | bytes 1179680 | tf_op jit(solution)/shard_map/ppermute | solution.py:53
  133.5 3.7 %add_convert_fusion.5 = (bf16[1,768,384]{2,1,0:T(8,128)(2,1)S(1)}, bf16[1,768,384]{2,1,0:T(8,128)(2,1)S(1)}, bf16[1,768,384]{2,1,0:T(8,128)(2,1)S(1)}, bf16[1,768,384]{2,1,0:T(8,128)(2,1)S(1)}) fusion(bf16[2,768,384]{2,1,0:T(8,128)(2,1)S(1)} %collective-permute-done.21, bf16[4,768,384]{2,1,0:T(8,128)(2,1)} %collective-permute-done.19, ...), kind=kLoop, calls=%fused_computation.22 | loop fusion | flops 7077888 | bytes 9437184 | tf_op jit(solution)/shard_map/convert_element_type | solution.py:254
  137.6 6.1 %keep_products.3 = (bf16[1,1024,384]{2,1,0:T(8,128)(2,1)S(1)}, bf16[3,1024,384]{2,1,0:T(8,128)(2,1)S(1)}) custom-call(s32[32]{0:T(128)S(1)} %dynamic-slice_bitcast_fusion.order, bf16[1024,768]{1,0:T(8,128)(2,1)S(1)} %copy-done.5, bf16[16,192,768]{2,1,0:T(8,128)(2,1)S(1)} %copy-done.3, bf16[16,192,768]{2,1,0:T(8,128)(2,1)S(1)} %copy-done.3, ...), custom_call_target="tpu_custom_call" | custom-call | flops 1 | bytes 1 | tf_op jit(solution)/shard_map/keep_products/pallas_call | solution.py:203
  143.8 1.6 collective-permute-start.16
  145.6 3.3 %collective-permute-start.23 = (bf16[2,384,384]{2,1,0:T(8,128)(2,1)S(1)}, bf16[2,384,384]{2,1,0:T(8,128)(2,1)S(1)}, u32[]{:S(2)}, u32[]{:S(2)}) collective-permute-start(bf16[2,384,384]{2,1,0:T(8,128)(2,1)S(1)} %pad_maximum_fusion.3), channel_id=1, source_target_pairs={{0,24},{1,97},{2,26},{3,99},{4,28},{5,101},{6,30},{7,103},{8,0},{9... | collective-permute-start | bytes 1769480 | tf_op jit(solution)/shard_map/ppermute | solution.py:53
  149.3 1.6 collective-permute-start.9
  151.6 1.4 collective-permute-start.28
  153.0 4.1 %collective-permute-done.16 = bf16[1024,384]{1,0:T(8,128)(2,1)S(1)} collective-permute-done((bf16[1024,384]{1,0:T(8,128)(2,1)S(1)}, bf16[1024,384]{1,0:T(8,128)(2,1)S(1)}, u32[]{:S(2)}, u32[]{:S(2)}) %collective-permute-start.16) | collective-permute-done | bytes 786464 | tf_op jit(solution)/shard_map/ppermute | solution.py:53
  157.8 3.3 %collective-permute-start.26 = (bf16[384,384]{1,0:T(8,128)(2,1)S(1)}, bf16[384,384]{1,0:T(8,128)(2,1)S(1)}, u32[]{:S(2)}, u32[]{:S(2)}) collective-permute-start(bf16[384,384]{1,0:T(8,128)(2,1)S(1)} %fusion.8), channel_id=1, source_target_pairs={{0,24},{1,97},{2,26},{3,99},{4,28},{5,101},{6,30},{7,103},{8,0},{9... | collective-permute-start | bytes 884744 | tf_op jit(solution)/shard_map/ppermute | solution.py:53
  161.2 4.2 %collective-permute-done.9 = bf16[1024,384]{1,0:T(8,128)(2,1)S(1)} collective-permute-done((bf16[1024,384]{1,0:T(8,128)(2,1)S(1)}, bf16[1024,384]{1,0:T(8,128)(2,1)S(1)}, u32[]{:S(2)}, u32[]{:S(2)}) %collective-permute-start.9) | collective-permute-done | bytes 786464 | tf_op jit(solution)/shard_map/ppermute | solution.py:53
  166.8 3.0 %collective-permute-start.29 = (f32[1,128]{1,0:T(1,128)S(1)}, f32[1,128]{1,0:T(1,128)S(1)}, u32[]{:S(2)}, u32[]{:S(2)}) collective-permute-start(f32[1,128]{1,0:T(1,128)S(1)} %fusion.12), channel_id=1, source_target_pairs={{0,4},{1,5},{2,6},{3,7},{4,0},{5,1},{6,2},{7,3},{8,12},{9,13},{10,... | collective-permute-start | bytes 1544 | tf_op jit(solution)/shard_map/ppermute | solution.py:53
  169.8 13.8 %collective-permute-done.29 = f32[1,128]{1,0:T(1,128)S(1)} collective-permute-done((f32[1,128]{1,0:T(1,128)S(1)}, f32[1,128]{1,0:T(1,128)S(1)}, u32[]{:S(2)}, u32[]{:S(2)}) %collective-permute-start.29) | collective-permute-done | bytes 544 | tf_op jit(solution)/shard_map/ppermute | solution.py:53
  183.6 4.9 %collective-permute-done.30 = f32[1,128]{1,0:T(1,128)S(1)} collective-permute-done((f32[1,128]{1,0:T(1,128)S(1)}, f32[1,128]{1,0:T(1,128)S(1)}, u32[]{:S(2)}, u32[]{:S(2)}) %collective-permute-start.30) | collective-permute-done | bytes 544 | tf_op jit(solution)/shard_map/ppermute | solution.py:53
  189.7 3.8 %collective-permute-done.31 = f32[1,128]{1,0:T(1,128)S(1)} collective-permute-done((f32[1,128]{1,0:T(1,128)S(1)}, f32[1,128]{1,0:T(1,128)S(1)}, u32[]{:S(2)}, u32[]{:S(2)}) %collective-permute-start.31) | collective-permute-done | bytes 544 | tf_op jit(solution)/shard_map/ppermute | solution.py:53
  193.5 1.8 collective-permute-start.32
  195.2 3.0 %collective-permute-done.32 = f32[1,128]{1,0:T(1,128)S(1)} collective-permute-done((f32[1,128]{1,0:T(1,128)S(1)}, f32[1,128]{1,0:T(1,128)S(1)}, u32[]{:S(2)}, u32[]{:S(2)}) %collective-permute-start.32) | collective-permute-done | bytes 544 | tf_op jit(solution)/shard_map/ppermute | solution.py:53
  198.2 1.3 collective-permute-start.33
  199.5 3.8 %collective-permute-done.33 = f32[1,128]{1,0:T(1,128)S(1)} collective-permute-done((f32[1,128]{1,0:T(1,128)S(1)}, f32[1,128]{1,0:T(1,128)S(1)}, u32[]{:S(2)}, u32[]{:S(2)}) %collective-permute-start.33) | collective-permute-done | bytes 544 | tf_op jit(solution)/shard_map/ppermute | solution.py:53
  204.7 1.4 copy.8
  206.1 1.3 fusion.5
  207.7 10.1 %collective-permute-done.18 = bf16[1024,384]{1,0:T(8,128)(2,1)S(1)} collective-permute-done((bf16[1024,384]{1,0:T(8,128)(2,1)}, bf16[1024,384]{1,0:T(8,128)(2,1)S(1)}, u32[]{:S(2)}, u32[]{:S(2)}) %collective-permute-start.18) | collective-permute-done | bytes 786464 | tf_op jit(solution)/shard_map/ppermute | solution.py:53
  217.8 1.3 fusion.2
  219.4 1.9 pad_maximum_fusion
  (122 shorter events, 15.6 us)
Async XLA Ops:
  0.6 34.9 %collective-permute-start.2 = (bf16[384,768]{1,0:T(8,128)(2,1)}, bf16[384,768]{1,0:T(8,128)(2,1)S(1)}, u32[]{:S(2)}, u32[]{:S(2)}) collective-permute-start(bf16[384,768]{1,0:T(8,128)(2,1)} %param.6), channel_id=1, source_target_pairs={{0,64},{1,17},{2,66},{3,19},{4,68},{5,21},{6,70},{7,23},{8,72},{9,... | collective-permute-start | bytes 1769480 | tf_op jit(solution)/shard_map/ppermute | solution.py:53
  3.8 33.7 %collective-permute-start = (bf16[384,768]{1,0:T(8,128)(2,1)}, bf16[384,768]{1,0:T(8,128)(2,1)S(1)}, u32[]{:S(2)}, u32[]{:S(2)}) collective-permute-start(bf16[384,768]{1,0:T(8,128)(2,1)} %param.6), channel_id=1, source_target_pairs={{0,32},{1,9},{2,34},{3,11},{4,36},{5,13},{6,38},{7,15},{8,40},{9,1... | collective-permute-start | bytes 1769480 | tf_op jit(solution)/shard_map/ppermute | solution.py:53
  4.4 33.1 %collective-permute-start.1 = (bf16[384,768]{1,0:T(8,128)(2,1)}, bf16[384,768]{1,0:T(8,128)(2,1)S(1)}, u32[]{:S(2)}, u32[]{:S(2)}) collective-permute-start(bf16[384,768]{1,0:T(8,128)(2,1)} %param.6), channel_id=1, source_target_pairs={{0,96},{1,25},{2,98},{3,27},{4,100},{5,29},{6,102},{7,31},{8,104},... | collective-permute-start | bytes 1769480 | tf_op jit(solution)/shard_map/ppermute | solution.py:53
  37.6 7.9 %copy-start.17 = (bf16[384,768]{1,0:T(8,128)(2,1)S(1)}, bf16[384,768]{1,0:T(8,128)(2,1)}, u32[]{:S(2)}) copy-start(bf16[384,768]{1,0:T(8,128)(2,1)} %param.6) | copy-start | bytes 1769476
  37.8 7.7 %copy-start.14 = (bf16[4,768,384]{2,1,0:T(8,128)(2,1)S(1)}, bf16[4,768,384]{2,1,0:T(8,128)(2,1)}, u32[]{:S(2)}) copy-start(bf16[4,768,384]{2,1,0:T(8,128)(2,1)} %copy-done.13) | copy-start | bytes 7077892
  37.8 18.3 %collective-permute-start.3 = (bf16[4,192,768]{2,1,0:T(8,128)(2,1)S(1)}, bf16[4,192,768]{2,1,0:T(8,128)(2,1)S(1)}, u32[]{:S(2)}, u32[]{:S(2)}) collective-permute-start(bf16[4,192,768]{2,1,0:T(8,128)(2,1)S(1)} %pad_maximum_fusion.1), channel_id=1, source_target_pairs={{0,8},{1,33},{2,10},{3,35},{4,12},{5,37},{6,14},{7,39},{8,16},{9,4... | collective-permute-start | bytes 3538952 | tf_op jit(solution)/shard_map/ppermute | solution.py:53
  39.8 28.0 %collective-permute-start.4 = (bf16[4,192,768]{2,1,0:T(8,128)(2,1)S(1)}, bf16[4,192,768]{2,1,0:T(8,128)(2,1)S(1)}, u32[]{:S(2)}, u32[]{:S(2)}) collective-permute-start(bf16[4,192,768]{2,1,0:T(8,128)(2,1)S(1)} %pad_maximum_fusion.1), channel_id=1, source_target_pairs={{0,24},{1,97},{2,26},{3,99},{4,28},{5,101},{6,30},{7,103},{8,0},{9... | collective-permute-start | bytes 3538952 | tf_op jit(solution)/shard_map/ppermute | solution.py:53
  42.1 31.1 %collective-permute-start.11 = (bf16[4,192,768]{2,1,0:T(8,128)(2,1)S(1)}, bf16[4,192,768]{2,1,0:T(8,128)(2,1)S(1)}, u32[]{:S(2)}, u32[]{:S(2)}) collective-permute-start(bf16[4,192,768]{2,1,0:T(8,128)(2,1)S(1)} %pad_maximum_fusion.2), channel_id=1, source_target_pairs={{0,8},{1,33},{2,10},{3,35},{4,12},{5,37},{6,14},{7,39},{8,16},{9,4... | collective-permute-start | bytes 3538952 | tf_op jit(solution)/shard_map/ppermute | solution.py:53
  42.2 50.8 %collective-permute-start.12 = (bf16[4,192,768]{2,1,0:T(8,128)(2,1)S(1)}, bf16[4,192,768]{2,1,0:T(8,128)(2,1)S(1)}, u32[]{:S(2)}, u32[]{:S(2)}) collective-permute-start(bf16[4,192,768]{2,1,0:T(8,128)(2,1)S(1)} %pad_maximum_fusion.2), channel_id=1, source_target_pairs={{0,24},{1,97},{2,26},{3,99},{4,28},{5,101},{6,30},{7,103},{8,0},{9... | collective-permute-start | bytes 3538952 | tf_op jit(solution)/shard_map/ppermute | solution.py:53
  45.4 66.8 %collective-permute-start.19 = (bf16[4,768,384]{2,1,0:T(8,128)(2,1)S(1)}, bf16[4,768,384]{2,1,0:T(8,128)(2,1)}, u32[]{:S(2)}, u32[]{:S(2)}) collective-permute-start(bf16[4,768,384]{2,1,0:T(8,128)(2,1)S(1)} %copy-done.14), channel_id=1, source_target_pairs={{0,96},{1,25},{2,98},{3,27},{4,100},{5,29},{6,102},{7,31},{8,104},... | collective-permute-start | bytes 7077896 | tf_op jit(solution)/shard_map/ppermute | solution.py:53
  45.5 22.2 %copy-start.12 = (bf16[4,768,384]{2,1,0:T(8,128)(2,1)S(1)}, bf16[4,768,384]{2,1,0:T(8,128)(2,1)}, u32[]{:S(2)}) copy-start(bf16[4,768,384]{2,1,0:T(8,128)(2,1)} %copy-done.11) | copy-start | bytes 7077892
  45.5 33.1 %copy-start.16 = (bf16[384,768]{1,0:T(8,128)(2,1)S(1)}, bf16[384,768]{1,0:T(8,128)(2,1)}, u32[]{:S(2)}) copy-start(bf16[384,768]{1,0:T(8,128)(2,1)} %tie.1) | copy-start | bytes 1769476
  56.1 39.5 %collective-permute-start.5 = (bf16[2,192,768]{2,1,0:T(8,128)(2,1)S(1)}, bf16[2,192,768]{2,1,0:T(8,128)(2,1)S(1)}, u32[]{:S(2)}, u32[]{:S(2)}) collective-permute-start(bf16[2,192,768]{2,1,0:T(8,128)(2,1)S(1)} %slice.227), channel_id=1, source_target_pairs={{0,8},{1,33},{2,10},{3,35},{4,12},{5,37},{6,14},{7,39},{8,16},{9,4... | collective-permute-start | bytes 1769480 | tf_op jit(solution)/shard_map/ppermute | solution.py:53
  67.7 44.5 %collective-permute-start.20 = (bf16[4,768,384]{2,1,0:T(8,128)(2,1)S(1)}, bf16[4,768,384]{2,1,0:T(8,128)(2,1)}, u32[]{:S(2)}, u32[]{:S(2)}) collective-permute-start(bf16[4,768,384]{2,1,0:T(8,128)(2,1)S(1)} %copy-done.12), channel_id=1, source_target_pairs={{0,32},{1,9},{2,34},{3,11},{4,36},{5,13},{6,38},{7,15},{8,40},{9,1... | collective-permute-start | bytes 7077896 | tf_op jit(solution)/shard_map/ppermute | solution.py:53
  73.2 27.0 %collective-permute-start.6 = (bf16[2,192,768]{2,1,0:T(8,128)(2,1)S(1)}, bf16[2,192,768]{2,1,0:T(8,128)(2,1)S(1)}, u32[]{:S(2)}, u32[]{:S(2)}) collective-permute-start(bf16[2,192,768]{2,1,0:T(8,128)(2,1)S(1)} %slice.228), channel_id=1, source_target_pairs={{0,24},{1,97},{2,26},{3,99},{4,28},{5,101},{6,30},{7,103},{8,0},{9... | collective-permute-start | bytes 1769480 | tf_op jit(solution)/shard_map/ppermute | solution.py:53
  93.0 13.6 %collective-permute-start.13 = (bf16[2,192,768]{2,1,0:T(8,128)(2,1)S(1)}, bf16[2,192,768]{2,1,0:T(8,128)(2,1)S(1)}, u32[]{:S(2)}, u32[]{:S(2)}) collective-permute-start(bf16[2,192,768]{2,1,0:T(8,128)(2,1)S(1)} %slice.233), channel_id=1, source_target_pairs={{0,8},{1,33},{2,10},{3,35},{4,12},{5,37},{6,14},{7,39},{8,16},{9,4... | collective-permute-start | bytes 1769480 | tf_op jit(solution)/shard_map/ppermute | solution.py:53
  95.6 11.1 %collective-permute-start.14 = (bf16[2,192,768]{2,1,0:T(8,128)(2,1)S(1)}, bf16[2,192,768]{2,1,0:T(8,128)(2,1)S(1)}, u32[]{:S(2)}, u32[]{:S(2)}) collective-permute-start(bf16[2,192,768]{2,1,0:T(8,128)(2,1)S(1)} %slice.234), channel_id=1, source_target_pairs={{0,24},{1,97},{2,26},{3,99},{4,28},{5,101},{6,30},{7,103},{8,0},{9... | collective-permute-start | bytes 1769480 | tf_op jit(solution)/shard_map/ppermute | solution.py:53
  97.0 3.4 %copy-start.5 = (bf16[1024,768]{1,0:T(8,128)(2,1)S(1)}, bf16[1024,768]{1,0:T(8,128)(2,1)}, u32[]{:S(2)}) copy-start(bf16[1024,768]{1,0:T(8,128)(2,1)} %g_ref.9) | copy-start | bytes 4718596
  100.2 5.6 %copy-start = (bf16[16,192,768]{2,1,0:T(8,128)(2,1)}, bf16[16,192,768]{2,1,0:T(8,128)(2,1)S(1)}, u32[]{:S(2)}) copy-start(bf16[16,192,768]{2,1,0:T(8,128)(2,1)S(1)} %constant_dynamic-update-slice_fusion.w0.w1) | copy-start | bytes 14155780
  105.9 15.0 %collective-permute-start.7 = (bf16[4,1024,384]{2,1,0:T(8,128)(2,1)}, bf16[4,1024,384]{2,1,0:T(8,128)(2,1)}, u32[]{:S(2)}, u32[]{:S(2)}) collective-permute-start(bf16[4,1024,384]{2,1,0:T(8,128)(2,1)} %give_products.2), channel_id=1, source_target_pairs={{0,1},{1,0},{2,3},{3,2},{4,5},{5,4},{6,7},{7,6},{8,9},{9,8},{10,11... | collective-permute-start | bytes 9437192 | tf_op jit(solution)/shard_map/ppermute | solution.py:53
  106.7 5.6 %slice-start = ((s8[4718592]{0:T(1024)(128)(4,1)}), s8[4194304]{0:T(1024)(128)(4,1)S(1)}, s32[]{:S(2)}) async-start(s8[4718592]{0:T(1024)(128)(4,1)} %bitcast.66), calls=%async_computation | async-start | bytes 8388608
  106.7 5.5 %copy-start.2 = (bf16[16,192,768]{2,1,0:T(8,128)(2,1)}, bf16[16,192,768]{2,1,0:T(8,128)(2,1)S(1)}, u32[]{:S(2)}) copy-start(bf16[16,192,768]{2,1,0:T(8,128)(2,1)S(1)} %constant_dynamic-update-slice_fusion.8.w0.w1) | copy-start | bytes 14155780
  106.7 5.5 %slice-start.1 = ((s8[4718592]{0:T(1024)(128)(4,1)}), s8[524288]{0:T(1024)(128)(4,1)S(1)}, s32[]{:S(2)}) async-start(s8[4718592]{0:T(1024)(128)(4,1)} %bitcast.66), calls=%async_computation.1 | async-start | bytes 1048576
  112.2 25.0 %collective-permute-start.15 = (bf16[4,1024,384]{2,1,0:T(8,128)(2,1)}, bf16[4,1024,384]{2,1,0:T(8,128)(2,1)}, u32[]{:S(2)}, u32[]{:S(2)}) collective-permute-start(bf16[4,1024,384]{2,1,0:T(8,128)(2,1)} %give_products.3), channel_id=1, source_target_pairs={{0,1},{1,0},{2,3},{3,2},{4,5},{5,4},{6,7},{7,6},{8,9},{9,8},{10,11... | collective-permute-start | bytes 9437192 | tf_op jit(solution)/shard_map/ppermute | solution.py:53
  112.3 6.9 %copy-start.10 = (f32[8,384]{1,0:T(8,128)S(1)}, f32[8,384]{1,0:T(8,128)}, u32[]{:S(2)}) copy-start(f32[8,384]{1,0:T(8,128)} %copy-done.9) | copy-start | bytes 36868
  115.9 17.6 %collective-permute-start.21 = (bf16[2,768,384]{2,1,0:T(8,128)(2,1)}, bf16[2,768,384]{2,1,0:T(8,128)(2,1)S(1)}, u32[]{:S(2)}, u32[]{:S(2)}) collective-permute-start(bf16[2,768,384]{2,1,0:T(8,128)(2,1)} %get-tuple-element.28), channel_id=1, source_target_pairs={{0,32},{1,9},{2,34},{3,11},{4,36},{5,13},{6,38},{7,15},{8,40},{9,1... | collective-permute-start | bytes 3538952 | tf_op jit(solution)/shard_map/ppermute | solution.py:53
  115.9 17.6 %collective-permute-start.22 = (bf16[2,768,384]{2,1,0:T(8,128)(2,1)}, bf16[2,768,384]{2,1,0:T(8,128)(2,1)}, u32[]{:S(2)}, u32[]{:S(2)}) collective-permute-start(bf16[2,768,384]{2,1,0:T(8,128)(2,1)} %get-tuple-element.29), channel_id=1, source_target_pairs={{0,96},{1,25},{2,98},{3,27},{4,100},{5,29},{6,102},{7,31},{8,104},... | collective-permute-start | bytes 3538952 | tf_op jit(solution)/shard_map/ppermute | solution.py:53
  120.4 30.6 %collective-permute-start.27 = (f32[1,128]{1,0:T(1,128)S(1)}, f32[1,128]{1,0:T(1,128)S(1)}, u32[]{:S(2)}, u32[]{:S(2)}) collective-permute-start(f32[1,128]{1,0:T(1,128)S(1)} %broadcast_in_dim.3), channel_id=1, source_target_pairs={{0,1},{1,0},{2,3},{3,2},{4,5},{5,4},{6,7},{7,6},{8,9},{9,8},{10,11... | collective-permute-start | bytes 1544 | tf_op jit(solution)/shard_map/ppermute | solution.py:53
  120.9 2.3 %copy-start.1 = (bf16[16,192,768]{2,1,0:T(8,128)(2,1)S(1)}, bf16[16,192,768]{2,1,0:T(8,128)(2,1)}, u32[]{:S(2)}) copy-start(bf16[16,192,768]{2,1,0:T(8,128)(2,1)} %copy-done) | copy-start | bytes 14155780
  129.4 36.1 %copy-start.7 = (bf16[3,1024,384]{2,1,0:T(8,128)(2,1)}, bf16[3,1024,384]{2,1,0:T(8,128)(2,1)S(1)}, u32[]{:S(2)}) copy-start(bf16[3,1024,384]{2,1,0:T(8,128)(2,1)S(1)} %get-tuple-element.12) | copy-start | bytes 7077892
  129.4 19.8 %collective-permute-start.8 = (bf16[1024,384]{1,0:T(8,128)(2,1)S(1)}, bf16[1024,384]{1,0:T(8,128)(2,1)S(1)}, u32[]{:S(2)}, u32[]{:S(2)}) collective-permute-start(bf16[1024,384]{1,0:T(8,128)(2,1)S(1)} %bitcast.68), channel_id=1, source_target_pairs={{0,2},{1,7},{2,4},{3,1},{4,6},{5,3},{6,0},{7,5},{8,10},{9,15},{10,... | collective-permute-start | bytes 2359304 | tf_op jit(solution)/shard_map/ppermute | solution.py:53
  133.5 4.1 %copy-start.3 = (bf16[16,192,768]{2,1,0:T(8,128)(2,1)S(1)}, bf16[16,192,768]{2,1,0:T(8,128)(2,1)}, u32[]{:S(2)}) copy-start(bf16[16,192,768]{2,1,0:T(8,128)(2,1)} %copy-done.2) | copy-start | bytes 14155780
  143.8 59.5 %copy-start.8 = (bf16[3,1024,384]{2,1,0:T(8,128)(2,1)}, bf16[3,1024,384]{2,1,0:T(8,128)(2,1)S(1)}, u32[]{:S(2)}) copy-start(bf16[3,1024,384]{2,1,0:T(8,128)(2,1)S(1)} %get-tuple-element.14) | copy-start | bytes 7077892
  143.8 13.3 %collective-permute-start.16 = (bf16[1024,384]{1,0:T(8,128)(2,1)S(1)}, bf16[1024,384]{1,0:T(8,128)(2,1)S(1)}, u32[]{:S(2)}, u32[]{:S(2)}) collective-permute-start(bf16[1024,384]{1,0:T(8,128)(2,1)S(1)} %bitcast.69), channel_id=1, source_target_pairs={{0,2},{1,7},{2,4},{3,1},{4,6},{5,3},{6,0},{7,5},{8,10},{9,15},{10,... | collective-permute-start | bytes 2359304 | tf_op jit(solution)/shard_map/ppermute | solution.py:53
  145.6 12.1 %collective-permute-start.23 = (bf16[2,384,384]{2,1,0:T(8,128)(2,1)S(1)}, bf16[2,384,384]{2,1,0:T(8,128)(2,1)S(1)}, u32[]{:S(2)}, u32[]{:S(2)}) collective-permute-start(bf16[2,384,384]{2,1,0:T(8,128)(2,1)S(1)} %pad_maximum_fusion.3), channel_id=1, source_target_pairs={{0,24},{1,97},{2,26},{3,99},{4,28},{5,101},{6,30},{7,103},{8,0},{9... | collective-permute-start | bytes 1769480 | tf_op jit(solution)/shard_map/ppermute | solution.py:53
  149.0 12.1 %collective-permute-start.24 = (bf16[2,384,384]{2,1,0:T(8,128)(2,1)S(1)}, bf16[2,384,384]{2,1,0:T(8,128)(2,1)S(1)}, u32[]{:S(2)}, u32[]{:S(2)}) collective-permute-start(bf16[2,384,384]{2,1,0:T(8,128)(2,1)S(1)} %pad_maximum_fusion.4), channel_id=1, source_target_pairs={{0,8},{1,33},{2,10},{3,35},{4,12},{5,37},{6,14},{7,39},{8,16},{9,4... | collective-permute-start | bytes 1769480 | tf_op jit(solution)/shard_map/ppermute | solution.py:53
  149.3 16.1 %collective-permute-start.9 = (bf16[1024,384]{1,0:T(8,128)(2,1)S(1)}, bf16[1024,384]{1,0:T(8,128)(2,1)S(1)}, u32[]{:S(2)}, u32[]{:S(2)}) collective-permute-start(bf16[1024,384]{1,0:T(8,128)(2,1)S(1)} %fusion.3), channel_id=1, source_target_pairs={{0,2},{1,7},{2,4},{3,1},{4,6},{5,3},{6,0},{7,5},{8,10},{9,15},{10,... | collective-permute-start | bytes 2359304 | tf_op jit(solution)/shard_map/ppermute | solution.py:53
  151.6 14.5 %collective-permute-start.28 = (f32[1,128]{1,0:T(1,128)S(1)}, f32[1,128]{1,0:T(1,128)S(1)}, u32[]{:S(2)}, u32[]{:S(2)}) collective-permute-start(f32[1,128]{1,0:T(1,128)S(1)} %broadcast_maximum_fusion), channel_id=1, source_target_pairs={{0,2},{1,3},{2,4},{3,5},{4,6},{5,7},{6,0},{7,1},{8,10},{9,11},{10,... | collective-permute-start | bytes 1544 | tf_op jit(solution)/shard_map/ppermute | solution.py:53
  157.2 46.0 %collective-permute-start.17 = (bf16[1024,384]{1,0:T(8,128)(2,1)S(1)}, bf16[1024,384]{1,0:T(8,128)(2,1)S(1)}, u32[]{:S(2)}, u32[]{:S(2)}) collective-permute-start(bf16[1024,384]{1,0:T(8,128)(2,1)S(1)} %fusion), channel_id=1, source_target_pairs={{0,2},{1,7},{2,4},{3,1},{4,6},{5,3},{6,0},{7,5},{8,10},{9,15},{10,... | collective-permute-start | bytes 2359304 | tf_op jit(solution)/shard_map/ppermute | solution.py:53
  157.8 46.6 %collective-permute-start.26 = (bf16[384,384]{1,0:T(8,128)(2,1)S(1)}, bf16[384,384]{1,0:T(8,128)(2,1)S(1)}, u32[]{:S(2)}, u32[]{:S(2)}) collective-permute-start(bf16[384,384]{1,0:T(8,128)(2,1)S(1)} %fusion.8), channel_id=1, source_target_pairs={{0,24},{1,97},{2,26},{3,99},{4,28},{5,101},{6,30},{7,103},{8,0},{9... | collective-permute-start | bytes 884744 | tf_op jit(solution)/shard_map/ppermute | solution.py:53
  161.2 43.2 %collective-permute-start.25 = (bf16[384,384]{1,0:T(8,128)(2,1)S(1)}, bf16[384,384]{1,0:T(8,128)(2,1)S(1)}, u32[]{:S(2)}, u32[]{:S(2)}) collective-permute-start(bf16[384,384]{1,0:T(8,128)(2,1)S(1)} %fusion.7), channel_id=1, source_target_pairs={{0,8},{1,33},{2,10},{3,35},{4,12},{5,37},{6,14},{7,39},{8,16},{9,4... | collective-permute-start | bytes 884744 | tf_op jit(solution)/shard_map/ppermute | solution.py:53
  165.7 40.4 %collective-permute-start.10 = (bf16[1024,384]{1,0:T(8,128)(2,1)S(1)}, bf16[1024,384]{1,0:T(8,128)(2,1)S(1)}, u32[]{:S(2)}, u32[]{:S(2)}) collective-permute-start(bf16[1024,384]{1,0:T(8,128)(2,1)S(1)} %fusion.4), channel_id=1, source_target_pairs={{0,2},{1,7},{2,4},{3,1},{4,6},{5,3},{6,0},{7,5},{8,10},{9,15},{10,... | collective-permute-start | bytes 2359304 | tf_op jit(solution)/shard_map/ppermute | solution.py:53
  166.8 16.8 %collective-permute-start.29 = (f32[1,128]{1,0:T(1,128)S(1)}, f32[1,128]{1,0:T(1,128)S(1)}, u32[]{:S(2)}, u32[]{:S(2)}) collective-permute-start(f32[1,128]{1,0:T(1,128)S(1)} %fusion.12), channel_id=1, source_target_pairs={{0,4},{1,5},{2,6},{3,7},{4,0},{5,1},{6,2},{7,3},{8,12},{9,13},{10,... | collective-permute-start | bytes 1544 | tf_op jit(solution)/shard_map/ppermute | solution.py:53
  183.6 4.9 %collective-permute-start.30 = (f32[1,128]{1,0:T(1,128)S(1)}, f32[1,128]{1,0:T(1,128)S(1)}, u32[]{:S(2)}, u32[]{:S(2)}) collective-permute-start(f32[1,128]{1,0:T(1,128)S(1)} %max.23), channel_id=1, source_target_pairs={{0,32},{1,33},{2,34},{3,35},{4,36},{5,37},{6,38},{7,39},{8,40},{9,... | collective-permute-start | bytes 1544 | tf_op jit(solution)/shard_map/ppermute | solution.py:53
  188.4 5.0 %collective-permute-start.31 = (f32[1,128]{1,0:T(1,128)S(1)}, f32[1,128]{1,0:T(1,128)S(1)}, u32[]{:S(2)}, u32[]{:S(2)}) collective-permute-start(f32[1,128]{1,0:T(1,128)S(1)} %max.24), channel_id=1, source_target_pairs={{0,64},{1,65},{2,66},{3,67},{4,68},{5,69},{6,70},{7,71},{8,72},{9,... | collective-permute-start | bytes 1544 | tf_op jit(solution)/shard_map/ppermute | solution.py:53
  193.5 4.8 %collective-permute-start.32 = (f32[1,128]{1,0:T(1,128)S(1)}, f32[1,128]{1,0:T(1,128)S(1)}, u32[]{:S(2)}, u32[]{:S(2)}) collective-permute-start(f32[1,128]{1,0:T(1,128)S(1)} %max.25), channel_id=1, source_target_pairs={{0,8},{1,9},{2,10},{3,11},{4,12},{5,13},{6,14},{7,15},{8,16},{9,17... | collective-permute-start | bytes 1544 | tf_op jit(solution)/shard_map/ppermute | solution.py:53
  198.2 5.0 %collective-permute-start.33 = (f32[1,128]{1,0:T(1,128)S(1)}, f32[1,128]{1,0:T(1,128)S(1)}, u32[]{:S(2)}, u32[]{:S(2)}) collective-permute-start(f32[1,128]{1,0:T(1,128)S(1)} %max.26), channel_id=1, source_target_pairs={{0,16},{1,17},{2,18},{3,19},{4,20},{5,21},{6,22},{7,23},{8,24},{9,... | collective-permute-start | bytes 1544 | tf_op jit(solution)/shard_map/ppermute | solution.py:53
  204.4 13.4 %collective-permute-start.18 = (bf16[1024,384]{1,0:T(8,128)(2,1)}, bf16[1024,384]{1,0:T(8,128)(2,1)S(1)}, u32[]{:S(2)}, u32[]{:S(2)}) collective-permute-start(bf16[1024,384]{1,0:T(8,128)(2,1)} %fusion.1), channel_id=1, source_target_pairs={{0,2},{1,7},{2,4},{3,1},{4,6},{5,3},{6,0},{7,5},{8,10},{9,15},{10,... | collective-permute-start | bytes 2359304 | tf_op jit(solution)/shard_map/ppermute | solution.py:53
  (7 other events, 9.2 us)

commit v2 on v1

v2 whole, which is shorter than its diff:
```python
import jax
import jax.numpy as jnp
import numpy as np
from jax import lax
from jax.experimental import pallas as pl
from jax.experimental.pallas import tpu as pltpu
from jax.sharding import PartitionSpec as P

F32, BF16 = jnp.float32, jnp.bfloat16
AXES = ("dp", "tensor")
NX, NY, NZ = 4, 4, 4


def permutation(move):
    pairs = []
    for x in range(NX):
        for z in range(NZ):
            for y in range(NY):
                for c in range(2):
                    to = move(x, y, z, c)
                    pairs.append((flat(x, y, z, c), flat(*to)))
    return pairs


def flat(x, y, z, c):
    return ((x % NX) * NZ + z % NZ) * NY * 2 + (y % NY) * 2 + c % 2


def step_along(second, d):
    def move(x, y, z, c):
        return (x + d, y, z, c) if (c ^ second) == 0 else (x, y, z + d, c)

    return permutation(move)


FIRST = {d: step_along(0, d) for d in (1, -1, 2)}
SECOND = {d: step_along(1, d) for d in (1, -1, 2)}
TURN = permutation(lambda x, y, z, c: (x + y, x, 2 * c + z % 2, z // 2))


def send(value, pairs):
    return lax.ppermute(value, AXES, pairs)


def add(*terms):
    total = terms[0].astype(F32)
    for term in terms[1:]:
        total = total + term.astype(F32)
    return total


W_ORDER = (
    [(2, 0), (2, 1), (1, 2), (1, 3)]
    + [(2, 2), (2, 3), (3, 0), (3, 1)]
    + [(1, 0), (1, 1), (3, 2), (3, 3)]
    + [(0, 0), (0, 1), (0, 2), (0, 3)]
)


def weight_kernel(order, x_ref, g_ref, *refs):
    *out_refs, peak_ref, gt_ref = refs
    n = pl.program_id(0)

    @pl.when(n == 0)
    def _():
        gt_ref[...] = g_ref[...].T
        peak_ref[...] = jnp.zeros_like(peak_ref)

    out = jnp.dot(gt_ref[...], x_ref[...], preferred_element_type=F32)
    rows, cols = out.shape
    peak_ref[...] = jnp.maximum(
        peak_ref[...], jnp.max(jnp.abs(out).reshape(rows // 8, 8, cols), axis=0)
    )
    low = out.astype(BF16)
    for i, out_ref in enumerate(out_refs):

        @pl.when(n // 4 == i)
        def _(out_ref=out_ref):
            out_ref[0] = low


def weight_products(order, base, arrays, x, g):
    tokens, d = x.shape
    cols = g.shape[1]
    rows = d // (NX * NZ)
    grid_spec = pltpu.PrefetchScalarGridSpec(
        num_scalar_prefetch=1,
        grid=(4 * arrays,),
        in_specs=[
            pl.BlockSpec((tokens, rows), lambda n, o: (0, o[base + n])),
            pl.BlockSpec((tokens, cols), lambda n, o: (0, 0)),
        ],
        out_specs=[
            pl.BlockSpec((1, cols, rows), lambda n, o, i=i: (jnp.clip(n - 4 * i, 0, 3), 0, 0))
            for i in range(arrays)
        ]
        + [pl.BlockSpec((8, rows), lambda n, o: (0, 0))],
        scratch_shapes=[pltpu.VMEM((cols, tokens), BF16)],
    )
    return pl.pallas_call(
        weight_kernel,
        grid_spec=grid_spec,
        out_shape=[jax.ShapeDtypeStruct((4, cols, rows), BF16)] * arrays
        + [jax.ShapeDtypeStruct((8, rows), F32)],
        compiler_params=pltpu.CompilerParams(vmem_limit_bytes=40 * 2**20),
        cost_estimate=pl.CostEstimate(
            flops=2 * tokens * cols * rows * 4 * arrays, bytes_accessed=2 * 4 * arrays * rows * (tokens + cols), transcendentals=0
        ),
        name="weight_products",
    )(order, x, g)


SLOTS = (0, 1, 3, 2)


def tables():
    rows = []
    for dp in range(NX * NZ):
        for t in range(NY * 2):
            x, z, y, c = dp // NZ, dp % NZ, t // 2, t % 2
            columns, halves, row = [], [], []
            for j in SLOTS:
                for i in SLOTS:
                    bx, bz = ((x - i) % NX, (z - j) % NZ) if c == 0 else ((x - j) % NX, (z - i) % NZ)
                    columns.append(2 * ((bx - y) % NY) + bz // 2)
                    halves.append(bz % 2)
            for first, second in W_ORDER:
                rx, rz = (first, second) if c == 0 else (second, first)
                row.append(((x + rx) % NX) * NZ + (z + rz) % NZ)
            rows.append(columns + halves + row)
    return np.array(rows, np.int32)


BLOCKS = NX * NZ
W_BASE = 2 * BLOCKS


def block_product(g_ref, w_refs, per_array):
    n = pl.program_id(0)
    w = w_refs[0][0]
    for q in range(1, len(w_refs)):
        w = jnp.where(n >= q * per_array, w_refs[q][0], w)
    return lax.dot_general(g_ref[0], w, (((1,), (1,)), ((), ())), preferred_element_type=F32)


def begin_kernel(order, g_ref, w0, w1, w2, sum_ref):
    n = pl.program_id(0)

    @pl.when(n == 0)
    def _():
        sum_ref[...] = jnp.zeros_like(sum_ref)

    sum_ref[order[BLOCKS + n]] += block_product(g_ref, (w0, w1, w2), 4)


def end_kernel(order, g_ref, w0, w1, begun_ref, out_ref, sum_ref):
    n = pl.program_id(0)

    @pl.when(n == 0)
    def _():
        sum_ref[...] = begun_ref[...]

    sum_ref[order[BLOCKS + 12 + n]] += block_product(g_ref, (w0, w1), 2)

    @pl.when(n == pl.num_programs(0) - 1)
    def _():
        half = sum_ref.shape[2]
        out_ref[:, :half] = sum_ref[0].astype(BF16)
        out_ref[:, half:] = sum_ref[1].astype(BF16)


def input_products(order, g, arrays, begun=None):
    tokens, k = g.shape[1:]
    per_array, rows = arrays[0].shape[:2]
    steps = per_array * len(arrays)
    first = 0 if begun is None else 12
    whole = (2, tokens, rows)
    in_specs = [pl.BlockSpec((1, tokens, k), lambda n, o: (o[first + n], 0, 0))]
    in_specs += [
        pl.BlockSpec((1, rows, k), lambda n, o, q=q: (jnp.clip(n - q * per_array, 0, per_array - 1), 0, 0))
        for q in range(len(arrays))
    ]
    args = [g, *arrays]
    if begun is None:
        out_specs = pl.BlockSpec(whole, lambda n, o: (0, 0, 0))
        out_shape = jax.ShapeDtypeStruct(whole, F32)
        scratch = []
    else:
        in_specs.append(pl.BlockSpec(whole, lambda n, o: (0, 0, 0)))
        args.append(begun)
        out_specs = pl.BlockSpec((tokens, 2 * rows), lambda n, o: (0, 0))
        out_shape = jax.ShapeDtypeStruct((tokens, 2 * rows), BF16)
        scratch = [pltpu.VMEM(whole, F32)]
    return pl.pallas_call(
        begin_kernel if begun is None else end_kernel,
        grid_spec=pltpu.PrefetchScalarGridSpec(
            num_scalar_prefetch=1, grid=(steps,), in_specs=in_specs, out_specs=out_specs, scratch_shapes=scratch
        ),
        out_shape=out_shape,
        compiler_params=pltpu.CompilerParams(vmem_limit_bytes=40 * 2**20),
        cost_estimate=pl.CostEstimate(
            flops=2 * steps * tokens * k * rows, bytes_accessed=2 * steps * k * (tokens + rows), transcendentals=0
        ),
        name="input_products",
    )(order, *args)


def tie_kernel(*refs):
    pass


def tie(value, *after):
    spec = pl.BlockSpec(memory_space=pl.ANY)
    return pl.pallas_call(
        tie_kernel,
        in_specs=[spec] * (1 + len(after)),
        out_specs=spec,
        out_shape=jax.ShapeDtypeStruct(value.shape, value.dtype),
        input_output_aliases={0: 0},
        cost_estimate=pl.CostEstimate(flops=1, bytes_accessed=1, transcendentals=0),
        name="tie",
    )(value, *after)


def per_device(x_in, g, w):
    dp = lax.axis_index("dp")
    t = lax.axis_index("tensor")
    table = tables()
    order = lax.dynamic_index_in_dim(jnp.asarray(table), dp * NY * 2 + t, 0, keepdims=False)

    turned = send(w, TURN)
    plus, peak_a = weight_products(order, W_BASE, 1, x_in, g)
    turned = tie(turned, peak_a)
    near = [turned, send(turned, FIRST[1]), send(turned, FIRST[-1]), send(turned, FIRST[2])]
    minus, peak_b = weight_products(order, W_BASE + 4, 1, x_in, g)
    low, high, peak_c = weight_products(order, W_BASE + 8, 2, x_in, g)
    near[3] = tie(near[3], peak_c)

    g_all = lax.all_gather(g, "tensor", axis=0)

    line = jnp.stack(near)
    up, down = send(line, SECOND[1]), send(line, SECOND[-1])
    u, v = send(plus, FIRST[1]), send(minus, FIRST[-1])

    peaks = lax.all_gather(jnp.maximum(jnp.maximum(peak_a, peak_b), peak_c), AXES)
    u = tie(u, up, down)

    far = [send(up[:2], SECOND[1]), send(down[2:], SECOND[-1])]
    r = send(add(low[0:2], u[0:2]).astype(BF16), FIRST[1])
    s = send(add(low[2:4], v[0:2]).astype(BF16), FIRST[-1])
    begun = input_products(order, g_all, [line, up, down])
    r = tie(r, begun, *far)

    e = [add(high[0], v[2], r[0]), add(high[1], v[3], r[1]), add(high[2], u[2], s[0]), add(high[3], u[3], s[1])]
    e = [b.astype(BF16) for b in e]
    h = e[0].shape[0] // 2
    u = send(jnp.stack([e[2][:h], e[1][h:]]), SECOND[1])
    v = send(jnp.stack([e[2][h:], e[3][:h]]), SECOND[-1])
    grad_peak = jnp.max(peaks)
    input_grad = input_products(order, g_all, far, begun)
    u = tie(u, input_grad, peaks)
    r = send(add(e[1][:h], u[0]).astype(BF16), SECOND[1])
    s = send(add(e[3][h:], v[0]).astype(BF16), SECOND[-1])
    total = jnp.concatenate([add(e[0][:h], v[1], r), add(e[0][h:], u[1], s)], axis=0)
    weight_grad = total.T / grad_peak
    return input_grad, weight_grad, grad_peak


def solution(mesh):
    return jax.shard_map(
        per_device,
        mesh=mesh,
        in_specs=(P("dp", None), P("dp", "tensor"), P("dp", "tensor")),
        out_specs=(P("dp", "tensor"), P("dp", "tensor"), P()),
        check_vma=False,
    )
```

time: 222 us -> 188 us (0.85)
  the two profiles are of different devices: /device:TPU:0 before, /device:TPU:16 now
where the time goes in v2:
time: 188 us; the launch traced here: 187 us
  Pallas kernels  51.5 us (27%)
  waiting for transfers between devices  43.4 us (23%)
  starting transfers between devices  38.8 us (21%)
  other arithmetic  19.6 us (10%)
  local copies, waits for them, and re-layouts  19.4 us (10%)
  between operations  14.2 us (8%)
    ppermute x16, waiting for transfers between devices, send(): return lax.ppermute(value, AXES, pairs)  42.7 us
    ppermute x16, starting transfers between devices, send(): return lax.ppermute(value, AXES, pairs)  38.7 us
    pallas_call x2, Pallas kernels, input_products(): pl.pallas_call(begin_kernel if begun is None else end_kernel, grid_spec=p...  26.5 us
    pallas_call x3, Pallas kernels, weight_products(): pl.pallas_call(weight_kernel, grid_spec=grid_spec, out_shape=[jax.ShapeDt...  25 us
    unnamed x43, local copies, waits for them, and re-layouts  13.9 us
    slice x2, local copies, waits for them, and re-layouts, per_device(): far = [send(up[:2], SECOND[1]), send(down[2:], SECOND[-1])]  4.72 us
    convert_element_type x1, other arithmetic, per_device(): r = send(add(low[0:2], u[0:2]).astype(BF16), FIRST[1])  4.29 us
    convert_element_type x1, other arithmetic, per_device(): e = [b.astype(BF16) for b in e]  3.96 us
  transfers between devices with their start and end apart: 18, of which 6 were waited for; matrix products, arithmetic and copies ran while one was open for 12% of the time, Pallas kernels for 28%

profile of v2, /device:TPU:16, one launch (start us, length us, event | category | flops | bytes accessed | tf_op | source)
XLA Modules:
  0.0 186.9 jit_solution(13615140649359261668)
XLA Ops:
  7.2 0.7 all-gather.5.cloned.1.call-update
  8.0 4.7 %collective-permute-start = (bf16[384,768]{1,0:T(8,128)(2,1)}, bf16[384,768]{1,0:T(8,128)(2,1)S(1)}, u32[]{:S(2)}, u32[]{:S(2)}) collective-permute-start(bf16[384,768]{1,0:T(8,128)(2,1)} %param.6), channel_id=1, source_target_pairs={{0,0},{1,16},{2,32},{3,48},{4,64},{5,80},{6,96},{7,112},{8,8},{9,2... | collective-permute-start | bytes 1769480 | tf_op jit(solution)/shard_map/ppermute | solution.py:42
  12.7 0.7 dynamic-slice_bitcast_fusion.order
  13.4 6.5 %weight_products.3 = (bf16[4,768,384]{2,1,0:T(8,128)(2,1)S(1)}, f32[8,384]{1,0:T(8,128)S(1)}) custom-call(s32[48]{0:T(128)S(1)} %dynamic-slice_bitcast_fusion.order, bf16[1024,6144]{1,0:T(8,128)(2,1)} %x_ref.5, bf16[1024,768]{1,0:T(8,128)(2,1)S(1)} %copy-done), custom_call_target="tpu_custom_call" | custom-call | flops 2415919104 | bytes 5505024 | tf_op jit(solution)/shard_map/weight_products/pallas_call | solution.py:100
  19.9 0.6 copy-done.9
  20.5 1.4 copy-done.13
  21.8 3.1 %collective-permute-done.refs_0_ = bf16[384,768]{1,0:T(8,128)(2,1)S(1)} collective-permute-done((bf16[384,768]{1,0:T(8,128)(2,1)}, bf16[384,768]{1,0:T(8,128)(2,1)S(1)}, u32[]{:S(2)}, u32[]{:S(2)}) %collective-permute-start) | collective-permute-done | bytes 589856 | tf_op jit(solution)/shard_map/ppermute | solution.py:42
  25.0 0.8 copy-done.16
  25.8 3.4 %collective-permute-start.3 = (bf16[384,768]{1,0:T(8,128)(2,1)}, bf16[384,768]{1,0:T(8,128)(2,1)S(1)}, u32[]{:S(2)}, u32[]{:S(2)}) collective-permute-start(bf16[384,768]{1,0:T(8,128)(2,1)} %tie.5), channel_id=1, source_target_pairs={{0,64},{1,17},{2,66},{3,19},{4,68},{5,21},{6,70},{7,23},{8,72},{9,... | collective-permute-start | bytes 1769480 | tf_op jit(solution)/shard_map/ppermute | solution.py:42
  29.3 1.9 %collective-permute-start.1 = (bf16[384,768]{1,0:T(8,128)(2,1)}, bf16[384,768]{1,0:T(8,128)(2,1)}, u32[]{:S(2)}, u32[]{:S(2)}) collective-permute-start(bf16[384,768]{1,0:T(8,128)(2,1)} %tie.5), channel_id=1, source_target_pairs={{0,32},{1,9},{2,34},{3,11},{4,36},{5,13},{6,38},{7,15},{8,40},{9,1... | collective-permute-start | bytes 1769480 | tf_op jit(solution)/shard_map/ppermute | solution.py:42
  31.3 11.0 %weight_products.4 = (bf16[4,768,384]{2,1,0:T(8,128)(2,1)S(1)}, bf16[4,768,384]{2,1,0:T(8,128)(2,1)S(1)}, f32[8,384]{1,0:T(8,128)S(1)}) custom-call(s32[48]{0:T(128)S(1)} %dynamic-slice_bitcast_fusion.order, bf16[1024,6144]{1,0:T(8,128)(2,1)} %x_ref.5, bf16[1024,768]{1,0:T(8,128)(2,1)S(1)} %copy-done), custom_call_target="tpu_custom_call" | custom-call | flops 4831838208 | bytes 11010048 | tf_op jit(solution)/shard_map/weight_products/pallas_call | solution.py:100
  42.2 1.4 copy-done.7
  43.7 1.4 copy-done.8
  45.1 0.6 copy-done.11
  45.7 0.8 copy-done.18
  46.5 0.5 copy-done.17
  47.0 3.0 %pad_maximum_fusion.w0 = bf16[4,384,768]{2,1,0:T(8,128)(2,1)} fusion(bf16[1,384,768]{2,1,0:T(8,128)(2,1)} %bitcast.22, bf16[1,384,768]{2,1,0:T(8,128)(2,1)S(1)} %bitcast.23, bf16[1,384,768]{2,1,0:T(8,128)(2,1)} %bitcast.3, bf16[1,384,768]{2,1,0:T(8,128)(2,1)S(1)} %bitcast.21), kind=kLoop, calls=%fused_computation | loop fusion | flops 3538944 | bytes 4718592 | tf_op jit(solution)/shard_map/stack | solution.py:241
  50.0 4.1 %collective-permute-start.4 = (bf16[4,384,768]{2,1,0:T(8,128)(2,1)}, bf16[4,384,768]{2,1,0:T(8,128)(2,1)}, u32[]{:S(2)}, u32[]{:S(2)}) collective-permute-start(bf16[4,384,768]{2,1,0:T(8,128)(2,1)} %pad_maximum_fusion.w0), channel_id=1, source_target_pairs={{0,8},{1,33},{2,10},{3,35},{4,12},{5,37},{6,14},{7,39},{8,16},{9,4... | collective-permute-start | bytes 7077896 | tf_op jit(solution)/shard_map/ppermute | solution.py:42
  54.1 7.9 %collective-permute-start.6 = (bf16[4,384,768]{2,1,0:T(8,128)(2,1)}, bf16[4,384,768]{2,1,0:T(8,128)(2,1)}, u32[]{:S(2)}, u32[]{:S(2)}) collective-permute-start(bf16[4,384,768]{2,1,0:T(8,128)(2,1)} %pad_maximum_fusion.w0), channel_id=1, source_target_pairs={{0,24},{1,97},{2,26},{3,99},{4,28},{5,101},{6,30},{7,103},{8,0},{9... | collective-permute-start | bytes 7077896 | tf_op jit(solution)/shard_map/ppermute | solution.py:42
  62.0 7.6 %weight_products.5 = (bf16[4,768,384]{2,1,0:T(8,128)(2,1)}, f32[8,384]{1,0:T(8,128)S(1)}) custom-call(s32[48]{0:T(128)S(1)} %dynamic-slice_bitcast_fusion.order, bf16[1024,6144]{1,0:T(8,128)(2,1)} %x_ref.5, bf16[1024,768]{1,0:T(8,128)(2,1)S(1)} %copy-done), custom_call_target="tpu_custom_call" | custom-call | flops 2415919104 | bytes 5505024 | tf_op jit(solution)/shard_map/weight_products/pallas_call | solution.py:100
  69.6 3.1 %collective-permute-start.8 = (bf16[4,768,384]{2,1,0:T(8,128)(2,1)}, bf16[4,768,384]{2,1,0:T(8,128)(2,1)}, u32[]{:S(2)}, u32[]{:S(2)}) collective-permute-start(bf16[4,768,384]{2,1,0:T(8,128)(2,1)} %get-tuple-element.13), channel_id=1, source_target_pairs={{0,96},{1,25},{2,98},{3,27},{4,100},{5,29},{6,102},{7,31},{8,104},... | collective-permute-start | bytes 7077896 | tf_op jit(solution)/shard_map/ppermute | solution.py:42
  72.7 0.6 maximum_maximum_fusion
  73.4 24.8 %collective-permute-done.4.w1.refs_1_ = bf16[4,384,768]{2,1,0:T(8,128)(2,1)} collective-permute-done((bf16[4,384,768]{2,1,0:T(8,128)(2,1)}, bf16[4,384,768]{2,1,0:T(8,128)(2,1)}, u32[]{:S(2)}, u32[]{:S(2)}) %collective-permute-start.4) | collective-permute-done | bytes 2359328 | tf_op jit(solution)/shard_map/ppermute | solution.py:42
  98.2 2.4 %slice.140 = bf16[2,384,768]{2,1,0:T(8,128)(2,1)} slice(bf16[4,384,768]{2,1,0:T(8,128)(2,1)} %collective-permute-done.4.w1.refs_1_), slice={[0:2], [0:384], [0:768]} | slice | bytes 2359296 | tf_op jit(solution)/shard_map/slice | solution.py:248
  100.6 10.8 %collective-permute-done.6.w2.refs_2_ = bf16[4,384,768]{2,1,0:T(8,128)(2,1)} collective-permute-done((bf16[4,384,768]{2,1,0:T(8,128)(2,1)}, bf16[4,384,768]{2,1,0:T(8,128)(2,1)}, u32[]{:S(2)}, u32[]{:S(2)}) %collective-permute-start.6) | collective-permute-done | bytes 2359328 | tf_op jit(solution)/shard_map/ppermute | solution.py:42
  111.4 2.4 %slice.141 = bf16[2,384,768]{2,1,0:T(8,128)(2,1)} slice(bf16[4,384,768]{2,1,0:T(8,128)(2,1)} %collective-permute-done.6.w2.refs_2_), slice={[2:4], [0:384], [0:768]} | slice | bytes 2359296 | tf_op jit(solution)/shard_map/slice | solution.py:248
  113.8 3.7 %collective-permute-start.7 = (bf16[2,384,768]{2,1,0:T(8,128)(2,1)}, bf16[2,384,768]{2,1,0:T(8,128)(2,1)S(1)}, u32[]{:S(2)}, u32[]{:S(2)}) collective-permute-start(bf16[2,384,768]{2,1,0:T(8,128)(2,1)} %slice.141), channel_id=1, source_target_pairs={{0,24},{1,97},{2,26},{3,99},{4,28},{5,101},{6,30},{7,103},{8,0},{9... | collective-permute-start | bytes 3538952 | tf_op jit(solution)/shard_map/ppermute | solution.py:42
  117.8 4.3 %add_convert_fusion.1 = (bf16[2,768,384]{2,1,0:T(8,128)(2,1)}, bf16[2,768,384]{2,1,0:T(8,128)(2,1)}) fusion(bf16[4,768,384]{2,1,0:T(8,128)(2,1)} %tie.7, bf16[4,768,384]{2,1,0:T(8,128)(2,1)} %copy-done.7, bf16[4,768,384]{2,1,0:T(8,128)(2,1)} %collective-permute-done.8), kind=kLoop, calls=%fused_computation.2 | loop fusion | flops 4718592 | bytes 7077888 | tf_op jit(solution)/shard_map/convert_element_type | solution.py:249
  122.1 1.9 %collective-permute-start.10 = (bf16[2,768,384]{2,1,0:T(8,128)(2,1)}, bf16[2,768,384]{2,1,0:T(8,128)(2,1)S(1)}, u32[]{:S(2)}, u32[]{:S(2)}) collective-permute-start(bf16[2,768,384]{2,1,0:T(8,128)(2,1)} %get-tuple-element.26), channel_id=1, source_target_pairs={{0,32},{1,9},{2,34},{3,11},{4,36},{5,13},{6,38},{7,15},{8,40},{9,1... | collective-permute-start | bytes 3538952 | tf_op jit(solution)/shard_map/ppermute | solution.py:42
  124.0 1.3 collective-permute-start.11
  125.3 18.4 %input_products.2.begun_ref.refs_1_ = f32[2,1024,384]{2,1,0:T(8,128)S(1)} custom-call(s32[48]{0:T(128)S(1)} %dynamic-slice_bitcast_fusion.order, bf16[8,1024,768]{2,1,0:T(8,128)(2,1)} %bitcast.18, bf16[4,384,768]{2,1,0:T(8,128)(2,1)} %pad_maximum_fusion.w0, bf16[4,384,768]{2,1,0:T(8,128)(2,1)} %collective-permute-done.4.w1.refs_1_, ...), custom_call_target="tpu_custom_call" | custom-call | flops 7247757312 | bytes 25952256 | tf_op jit(solution)/shard_map/input_products/pallas_call | solution.py:194
  143.7 1.6 copy-done.1
  145.4 1.0 copy-done.3
  146.7 1.1 copy-done.15
  147.9 4.0 %add_convert_fusion.5 = (bf16[1,768,384]{2,1,0:T(8,128)(2,1)S(1)}, bf16[1,768,384]{2,1,0:T(8,128)(2,1)S(1)}, bf16[1,768,384]{2,1,0:T(8,128)(2,1)S(1)}, bf16[1,768,384]{2,1,0:T(8,128)(2,1)S(1)}) fusion(bf16[2,768,384]{2,1,0:T(8,128)(2,1)} %tie.8, bf16[4,768,384]{2,1,0:T(8,128)(2,1)} %collective-permute-done.8, bf16[4,768,384]{2,1,0:T(8,128)(2,1)} %copy-done.8, ...), kind=kLoop, calls=%fused_computation.8 | loop fusion | flops 7077888 | bytes 9437184 | tf_op jit(solution)/shard_map/convert_element_type | solution.py:255
  152.2 0.9 pad_maximum_fusion.1
  153.1 3.2 %collective-permute-start.12 = (bf16[2,384,384]{2,1,0:T(8,128)(2,1)}, bf16[2,384,384]{2,1,0:T(8,128)(2,1)}, u32[]{:S(2)}, u32[]{:S(2)}) collective-permute-start(bf16[2,384,384]{2,1,0:T(8,128)(2,1)} %pad_maximum_fusion.1), channel_id=1, source_target_pairs={{0,24},{1,97},{2,26},{3,99},{4,28},{5,101},{6,30},{7,103},{8,0},{9... | collective-permute-start | bytes 1769480 | tf_op jit(solution)/shard_map/ppermute | solution.py:42
  156.3 8.1 %input_products.3.refs_1_ = bf16[1024,768]{1,0:T(8,128)(2,1)} custom-call(s32[48]{0:T(128)S(1)} %dynamic-slice_bitcast_fusion.order, bf16[8,1024,768]{2,1,0:T(8,128)(2,1)} %bitcast.19, bf16[2,384,768]{2,1,0:T(8,128)(2,1)S(1)} %copy-done.4, bf16[2,384,768]{2,1,0:T(8,128)(2,1)S(1)} %copy-done.6, f32[2,1024,384]{2,1,0:T(8,128)S(1)} %copy-done.2), custom_call_target="tpu_custom_call" | custom-call | flops 2415919104 | bytes 8650752 | tf_op jit(solution)/shard_map/input_products/pallas_call | solution.py:194
  164.4 0.8 copy-done.19
  165.2 1.9 %fusion.1 = bf16[384,384]{1,0:T(8,128)(2,1)} fusion(bf16[2,384,384]{2,1,0:T(8,128)(2,1)} %tie.9, bf16[1,768,384]{2,1,0:T(8,128)(2,1)S(1)} %get-tuple-element.21), kind=kLoop, calls=%fused_computation.15 | loop fusion | flops 589824 | bytes 884736 | tf_op jit(solution)/shard_map/convert_element_type | solution.py:262
  167.1 1.8 fusion.2
  168.9 3.2 %collective-permute-start.15 = (bf16[384,384]{1,0:T(8,128)(2,1)}, bf16[384,384]{1,0:T(8,128)(2,1)S(1)}, u32[]{:S(2)}, u32[]{:S(2)}) collective-permute-start(bf16[384,384]{1,0:T(8,128)(2,1)} %fusion.2), channel_id=1, source_target_pairs={{0,24},{1,97},{2,26},{3,99},{4,28},{5,101},{6,30},{7,103},{8,0},{9... | collective-permute-start | bytes 884744 | tf_op jit(solution)/shard_map/ppermute | solution.py:42
  172.1 1.0 reduce_max.9
  173.1 2.3 %collective-permute-done.14 = bf16[384,384]{1,0:T(8,128)(2,1)} collective-permute-done((bf16[384,384]{1,0:T(8,128)(2,1)}, bf16[384,384]{1,0:T(8,128)(2,1)}, u32[]{:S(2)}, u32[]{:S(2)}) %collective-permute-start.14) | collective-permute-done | bytes 294944 | tf_op jit(solution)/shard_map/ppermute | solution.py:42
  175.4 1.3 collective-permute-done.15
  176.7 1.3 bitcast_add_fusion.1
  177.9 0.7 fusion
  178.7 1.4 copy.12
  (60 shorter events, 1.3 us)
Async XLA Ops:
  7.2 6.2 %copy-start = (bf16[1024,768]{1,0:T(8,128)(2,1)S(1)}, bf16[1024,768]{1,0:T(8,128)(2,1)}, u32[]{:S(2)}) copy-start(bf16[1024,768]{1,0:T(8,128)(2,1)} %g_ref.5) | copy-start | bytes 4718596
  7.2 118.1 %all-gather.5.cloned.1.call-start = ((), (), s32[]{:S(2)}) async-start(), calls=%async_computation | async-start | bytes 14155776 | tf_op jit(solution)/shard_map/all_gather | solution.py:239
  7.9 156.5 %all-gather.7.cloned.1.call-start = ((), (), s32[]{:S(2)}) async-start(), calls=%async_computation.1 | async-start | bytes 1585152 | tf_op jit(solution)/shard_map/all_gather | solution.py:245
  8.0 17.0 %collective-permute-start = (bf16[384,768]{1,0:T(8,128)(2,1)}, bf16[384,768]{1,0:T(8,128)(2,1)S(1)}, u32[]{:S(2)}, u32[]{:S(2)}) collective-permute-start(bf16[384,768]{1,0:T(8,128)(2,1)} %param.6), channel_id=1, source_target_pairs={{0,0},{1,16},{2,32},{3,48},{4,64},{5,80},{6,96},{7,112},{8,8},{9,2... | collective-permute-start | bytes 1769480 | tf_op jit(solution)/shard_map/ppermute | solution.py:42
  19.9 0.6 copy-start.9
  20.5 1.4 copy-start.13
  25.0 0.8 copy-start.16
  25.8 19.9 %collective-permute-start.3 = (bf16[384,768]{1,0:T(8,128)(2,1)}, bf16[384,768]{1,0:T(8,128)(2,1)S(1)}, u32[]{:S(2)}, u32[]{:S(2)}) collective-permute-start(bf16[384,768]{1,0:T(8,128)(2,1)} %tie.5), channel_id=1, source_target_pairs={{0,64},{1,17},{2,66},{3,19},{4,68},{5,21},{6,70},{7,23},{8,72},{9,... | collective-permute-start | bytes 1769480 | tf_op jit(solution)/shard_map/ppermute | solution.py:42
  29.2 17.3 %collective-permute-start.2 = (bf16[384,768]{1,0:T(8,128)(2,1)}, bf16[384,768]{1,0:T(8,128)(2,1)S(1)}, u32[]{:S(2)}, u32[]{:S(2)}) collective-permute-start(bf16[384,768]{1,0:T(8,128)(2,1)} %tie.5), channel_id=1, source_target_pairs={{0,96},{1,25},{2,98},{3,27},{4,100},{5,29},{6,102},{7,31},{8,104},... | collective-permute-start | bytes 1769480 | tf_op jit(solution)/shard_map/ppermute | solution.py:42
  29.3 17.2 %collective-permute-start.1 = (bf16[384,768]{1,0:T(8,128)(2,1)}, bf16[384,768]{1,0:T(8,128)(2,1)}, u32[]{:S(2)}, u32[]{:S(2)}) collective-permute-start(bf16[384,768]{1,0:T(8,128)(2,1)} %tie.5), channel_id=1, source_target_pairs={{0,32},{1,9},{2,34},{3,11},{4,36},{5,13},{6,38},{7,15},{8,40},{9,1... | collective-permute-start | bytes 1769480 | tf_op jit(solution)/shard_map/ppermute | solution.py:42
  31.2 86.2 %collective-permute-start.9 = (bf16[4,768,384]{2,1,0:T(8,128)(2,1)}, bf16[4,768,384]{2,1,0:T(8,128)(2,1)}, u32[]{:S(2)}, u32[]{:S(2)}) collective-permute-start(bf16[4,768,384]{2,1,0:T(8,128)(2,1)} %copy-done.13), channel_id=1, source_target_pairs={{0,32},{1,9},{2,34},{3,11},{4,36},{5,13},{6,38},{7,15},{8,40},{9,1... | collective-permute-start | bytes 7077896 | tf_op jit(solution)/shard_map/ppermute | solution.py:42
  42.2 1.4 copy-start.7
  43.7 1.4 copy-start.8
  45.1 0.6 copy-start.11
  45.7 1.3 copy-start.17
  45.7 0.8 copy-start.18
  50.0 22.8 %copy-start.10 = (f32[8,384]{1,0:T(8,128)S(1)}, f32[8,384]{1,0:T(8,128)}, u32[]{:S(2)}) copy-start(f32[8,384]{1,0:T(8,128)} %copy-done.9) | copy-start | bytes 36868
  50.0 22.8 %copy-start.12 = (f32[8,384]{1,0:T(8,128)S(1)}, f32[8,384]{1,0:T(8,128)}, u32[]{:S(2)}) copy-start(f32[8,384]{1,0:T(8,128)} %copy-done.11) | copy-start | bytes 36868
  50.0 48.2 %collective-permute-start.4 = (bf16[4,384,768]{2,1,0:T(8,128)(2,1)}, bf16[4,384,768]{2,1,0:T(8,128)(2,1)}, u32[]{:S(2)}, u32[]{:S(2)}) collective-permute-start(bf16[4,384,768]{2,1,0:T(8,128)(2,1)} %pad_maximum_fusion.w0), channel_id=1, source_target_pairs={{0,8},{1,33},{2,10},{3,35},{4,12},{5,37},{6,14},{7,39},{8,16},{9,4... | collective-permute-start | bytes 7077896 | tf_op jit(solution)/shard_map/ppermute | solution.py:42
  54.1 57.3 %collective-permute-start.6 = (bf16[4,384,768]{2,1,0:T(8,128)(2,1)}, bf16[4,384,768]{2,1,0:T(8,128)(2,1)}, u32[]{:S(2)}, u32[]{:S(2)}) collective-permute-start(bf16[4,384,768]{2,1,0:T(8,128)(2,1)} %pad_maximum_fusion.w0), channel_id=1, source_target_pairs={{0,24},{1,97},{2,26},{3,99},{4,28},{5,101},{6,30},{7,103},{8,0},{9... | collective-permute-start | bytes 7077896 | tf_op jit(solution)/shard_map/ppermute | solution.py:42
  69.6 48.1 %collective-permute-start.8 = (bf16[4,768,384]{2,1,0:T(8,128)(2,1)}, bf16[4,768,384]{2,1,0:T(8,128)(2,1)}, u32[]{:S(2)}, u32[]{:S(2)}) collective-permute-start(bf16[4,768,384]{2,1,0:T(8,128)(2,1)} %get-tuple-element.13), channel_id=1, source_target_pairs={{0,96},{1,25},{2,98},{3,27},{4,100},{5,29},{6,102},{7,31},{8,104},... | collective-permute-start | bytes 7077896 | tf_op jit(solution)/shard_map/ppermute | solution.py:42
  100.6 44.8 %collective-permute-start.5 = (bf16[2,384,768]{2,1,0:T(8,128)(2,1)}, bf16[2,384,768]{2,1,0:T(8,128)(2,1)S(1)}, u32[]{:S(2)}, u32[]{:S(2)}) collective-permute-start(bf16[2,384,768]{2,1,0:T(8,128)(2,1)} %slice.140), channel_id=1, source_target_pairs={{0,8},{1,33},{2,10},{3,35},{4,12},{5,37},{6,14},{7,39},{8,16},{9,4... | collective-permute-start | bytes 3538952 | tf_op jit(solution)/shard_map/ppermute | solution.py:42
  113.8 31.6 %collective-permute-start.7 = (bf16[2,384,768]{2,1,0:T(8,128)(2,1)}, bf16[2,384,768]{2,1,0:T(8,128)(2,1)S(1)}, u32[]{:S(2)}, u32[]{:S(2)}) collective-permute-start(bf16[2,384,768]{2,1,0:T(8,128)(2,1)} %slice.141), channel_id=1, source_target_pairs={{0,24},{1,97},{2,26},{3,99},{4,28},{5,101},{6,30},{7,103},{8,0},{9... | collective-permute-start | bytes 3538952 | tf_op jit(solution)/shard_map/ppermute | solution.py:42
  122.1 23.3 %collective-permute-start.10 = (bf16[2,768,384]{2,1,0:T(8,128)(2,1)}, bf16[2,768,384]{2,1,0:T(8,128)(2,1)S(1)}, u32[]{:S(2)}, u32[]{:S(2)}) collective-permute-start(bf16[2,768,384]{2,1,0:T(8,128)(2,1)} %get-tuple-element.26), channel_id=1, source_target_pairs={{0,32},{1,9},{2,34},{3,11},{4,36},{5,13},{6,38},{7,15},{8,40},{9,1... | collective-permute-start | bytes 3538952 | tf_op jit(solution)/shard_map/ppermute | solution.py:42
  124.0 23.9 %collective-permute-start.11 = (bf16[2,768,384]{2,1,0:T(8,128)(2,1)}, bf16[2,768,384]{2,1,0:T(8,128)(2,1)}, u32[]{:S(2)}, u32[]{:S(2)}) collective-permute-start(bf16[2,768,384]{2,1,0:T(8,128)(2,1)} %get-tuple-element.27), channel_id=1, source_target_pairs={{0,96},{1,25},{2,98},{3,27},{4,100},{5,29},{6,102},{7,31},{8,104},... | collective-permute-start | bytes 3538952 | tf_op jit(solution)/shard_map/ppermute | solution.py:42
  143.7 1.7 copy-start.1
  145.3 1.0 copy-start.3
  145.3 1.4 copy-start.5
  146.7 1.1 copy-start.15
  147.9 8.4 %copy-start.6 = (bf16[2,384,768]{2,1,0:T(8,128)(2,1)S(1)}, bf16[2,384,768]{2,1,0:T(8,128)(2,1)}, u32[]{:S(2)}) copy-start(bf16[2,384,768]{2,1,0:T(8,128)(2,1)} %copy-done.5) | copy-start | bytes 3538948
  151.8 4.5 %copy-start.4 = (bf16[2,384,768]{2,1,0:T(8,128)(2,1)S(1)}, bf16[2,384,768]{2,1,0:T(8,128)(2,1)}, u32[]{:S(2)}) copy-start(bf16[2,384,768]{2,1,0:T(8,128)(2,1)} %copy-done.3) | copy-start | bytes 3538948
  151.9 4.4 %copy-start.2 = (f32[2,1024,384]{2,1,0:T(8,128)S(1)}, f32[2,1024,384]{2,1,0:T(8,128)}, u32[]{:S(2)}) copy-start(f32[2,1024,384]{2,1,0:T(8,128)} %copy-done.1) | copy-start | bytes 9437188
  152.0 12.4 %collective-permute-start.13 = (bf16[2,384,384]{2,1,0:T(8,128)(2,1)S(1)}, bf16[2,384,384]{2,1,0:T(8,128)(2,1)S(1)}, u32[]{:S(2)}, u32[]{:S(2)}) collective-permute-start(bf16[2,384,384]{2,1,0:T(8,128)(2,1)S(1)} %pad_maximum_fusion.2), channel_id=1, source_target_pairs={{0,8},{1,33},{2,10},{3,35},{4,12},{5,37},{6,14},{7,39},{8,16},{9,4... | collective-permute-start | bytes 1769480 | tf_op jit(solution)/shard_map/ppermute | solution.py:42
  153.1 14.0 %collective-permute-start.12 = (bf16[2,384,384]{2,1,0:T(8,128)(2,1)}, bf16[2,384,384]{2,1,0:T(8,128)(2,1)}, u32[]{:S(2)}, u32[]{:S(2)}) collective-permute-start(bf16[2,384,384]{2,1,0:T(8,128)(2,1)} %pad_maximum_fusion.1), channel_id=1, source_target_pairs={{0,24},{1,97},{2,26},{3,99},{4,28},{5,101},{6,30},{7,103},{8,0},{9... | collective-permute-start | bytes 1769480 | tf_op jit(solution)/shard_map/ppermute | solution.py:42
  164.4 0.8 copy-start.19
  165.2 6.9 %copy-start.14 = (f32[1024,384]{1,0:T(8,128)S(1)}, f32[1024,384]{1,0:T(8,128)}, u32[]{:S(2)}) copy-start(f32[1024,384]{1,0:T(8,128)} %all-gather.7.cloned.1.call-done) | copy-start | bytes 4718596
  167.1 9.6 %copy-start.20 = (bf16[2,384,384]{2,1,0:T(8,128)(2,1)S(1)}, bf16[2,384,384]{2,1,0:T(8,128)(2,1)}, u32[]{:S(2)}) copy-start(bf16[2,384,384]{2,1,0:T(8,128)(2,1)} %tie.9) | copy-start | bytes 1769476
  167.1 8.2 %collective-permute-start.14 = (bf16[384,384]{1,0:T(8,128)(2,1)}, bf16[384,384]{1,0:T(8,128)(2,1)}, u32[]{:S(2)}, u32[]{:S(2)}) collective-permute-start(bf16[384,384]{1,0:T(8,128)(2,1)} %fusion.1), channel_id=1, source_target_pairs={{0,8},{1,33},{2,10},{3,35},{4,12},{5,37},{6,14},{7,39},{8,16},{9,4... | collective-permute-start | bytes 884744 | tf_op jit(solution)/shard_map/ppermute | solution.py:42
  168.9 7.7 %collective-permute-start.15 = (bf16[384,384]{1,0:T(8,128)(2,1)}, bf16[384,384]{1,0:T(8,128)(2,1)S(1)}, u32[]{:S(2)}, u32[]{:S(2)}) collective-permute-start(bf16[384,384]{1,0:T(8,128)(2,1)} %fusion.2), channel_id=1, source_target_pairs={{0,24},{1,97},{2,26},{3,99},{4,28},{5,101},{6,30},{7,103},{8,0},{9... | collective-permute-start | bytes 884744 | tf_op jit(solution)/shard_map/ppermute | solution.py:42
Sparse Core Ops, SparseCore 0:
  9.7 70.2 all-gather.4
  82.8 65.1 all-gather.6

commit v3 on v2

--- a/solution.py
+++ b/solution.py
@@ -1,3 +1,5 @@
+import functools
+
 import jax
 import jax.numpy as jnp
 import numpy as np
@@ -143,37 +145,41 @@
     return lax.dot_general(g_ref[0], w, (((1,), (1,)), ((), ())), preferred_element_type=F32)
 
 
-def begin_kernel(order, g_ref, w0, w1, w2, sum_ref):
+def input_kernel(first, last, order, g_ref, *refs):
     n = pl.program_id(0)
-
-    @pl.when(n == 0)
-    def _():
-        sum_ref[...] = jnp.zeros_like(sum_ref)
-
-    sum_ref[order[BLOCKS + n]] += block_product(g_ref, (w0, w1, w2), 4)
-
-
-def end_kernel(order, g_ref, w0, w1, begun_ref, out_ref, sum_ref):
-    n = pl.program_id(0)
-
-    @pl.when(n == 0)
-    def _():
-        sum_ref[...] = begun_ref[...]
-
-    sum_ref[order[BLOCKS + 12 + n]] += block_product(g_ref, (w0, w1), 2)
-
-    @pl.when(n == pl.num_programs(0) - 1)
-    def _():
-        half = sum_ref.shape[2]
-        out_ref[:, :half] = sum_ref[0].astype(BF16)
-        out_ref[:, half:] = sum_ref[1].astype(BF16)
-
-
-def input_products(order, g, arrays, begun=None):
+    sum_ref = refs[-1]
+    if first == 0:
+        w_refs = refs[:-1]
+
+        @pl.when(n == 0)
+        def _():
+            sum_ref[...] = jnp.zeros_like(sum_ref)
+
+    else:
+        w_refs, begun_ref = refs[: -3 if last else -2], refs[-3 if last else -2]
+
+        @pl.when(n == 0)
+        def _():
+            sum_ref[...] = begun_ref[...]
+
+    per_array = 2 if last else 4
+    sum_ref[order[BLOCKS + first + n]] += block_product(g_ref, w_refs, per_array)
+
+    if last:
+        out_ref = refs[-2]
+
+        @pl.when(n == pl.num_programs(0) - 1)
+        def _():
+            half = sum_ref.shape[2]
+            out_ref[:, :half] = sum_ref[0].astype(BF16)
+            out_ref[:, half:] = sum_ref[1].astype(BF16)
+
+
+def input_products(order, first, g, arrays, begun=None):
     tokens, k = g.shape[1:]
     per_array, rows = arrays[0].shape[:2]
     steps = per_array * len(arrays)
-    first = 0 if begun is None else 12
+    last = first + steps == BLOCKS
     whole = (2, tokens, rows)
     in_specs = [pl.BlockSpec((1, tokens, k), lambda n, o: (o[first + n], 0, 0))]
     in_specs += [
@@ -181,20 +187,23 @@
         for q in range(len(arrays))
     ]
     args = [g, *arrays]
-    if begun is None:
+    if begun is not None:
+        in_specs.append(pl.BlockSpec(whole, lambda n, o: (0, 0, 0)))
+        args.append(begun)
+    if last:
+        out_specs = pl.BlockSpec((tokens, 2 * rows), lambda n, o: (0, 0))
+        out_shape = jax.ShapeDtypeStruct((tokens, 2 * rows), BF16)
+    else:
         out_specs = pl.BlockSpec(whole, lambda n, o: (0, 0, 0))
         out_shape = jax.ShapeDtypeStruct(whole, F32)
-        scratch = []
-    else:
-        in_specs.append(pl.BlockSpec(whole, lambda n, o: (0, 0, 0)))
-        args.append(begun)
-        out_specs = pl.BlockSpec((tokens, 2 * rows), lambda n, o: (0, 0))
-        out_shape = jax.ShapeDtypeStruct((tokens, 2 * rows), BF16)
-        scratch = [pltpu.VMEM(whole, F32)]
     return pl.pallas_call(
-        begin_kernel if begun is None else end_kernel,
+        functools.partial(input_kernel, first, last),
         grid_spec=pltpu.PrefetchScalarGridSpec(
-            num_scalar_prefetch=1, grid=(steps,), in_specs=in_specs, out_specs=out_specs, scratch_shapes=scratch
+            num_scalar_prefetch=1,
+            grid=(steps,),
+            in_specs=in_specs,
+            out_specs=out_specs,
+            scratch_shapes=[pltpu.VMEM(whole, F32)] if last else [],
         ),
         out_shape=out_shape,
         compiler_params=pltpu.CompilerParams(vmem_limit_bytes=40 * 2**20),
@@ -242,13 +251,14 @@
     up, down = send(line, SECOND[1]), send(line, SECOND[-1])
     u, v = send(plus, FIRST[1]), send(minus, FIRST[-1])
 
-    peaks = lax.all_gather(jnp.maximum(jnp.maximum(peak_a, peak_b), peak_c), AXES)
+    begun = input_products(order, 0, g_all, [line])
+    peaks = lax.all_gather(tie(jnp.maximum(jnp.maximum(peak_a, peak_b), peak_c), begun), AXES)
     u = tie(u, up, down)
 
     far = [send(up[:2], SECOND[1]), send(down[2:], SECOND[-1])]
     r = send(add(low[0:2], u[0:2]).astype(BF16), FIRST[1])
     s = send(add(low[2:4], v[0:2]).astype(BF16), FIRST[-1])
-    begun = input_products(order, g_all, [line, up, down])
+    begun = input_products(order, 4, g_all, [up, down], begun)
     r = tie(r, begun, *far)
 
     e = [add(high[0], v[2], r[0]), add(high[1], v[3], r[1]), add(high[2], u[2], s[0]), add(high[3], u[3], s[1])]
@@ -257,7 +267,7 @@
     u = send(jnp.stack([e[2][:h], e[1][h:]]), SECOND[1])
     v = send(jnp.stack([e[2][h:], e[3][:h]]), SECOND[-1])
     grad_peak = jnp.max(peaks)
-    input_grad = input_products(order, g_all, far, begun)
+    input_grad = input_products(order, 12, g_all, far, begun)
     u = tie(u, input_grad, peaks)
     r = send(add(e[1][:h], u[0]).astype(BF16), SECOND[1])
     s = send(add(e[3][h:], v[0]).astype(BF16), SECOND[-1])

time: 188 us -> 203 us (1.080)
  the two profiles are of different devices: /device:TPU:16 before, /device:TPU:0 now
where the time goes in v3:
time: 203 us; the launch traced here: 201 us
  waiting for transfers between devices  61.9 us (30%)
  Pallas kernels  52.6 us (26%)
  starting transfers between devices  39.3 us (19%)
  other arithmetic  16.9 us (8%)
  local copies, waits for them, and re-layouts  16.5 us (8%)
  between operations  14.3 us (7%)
    ppermute x16, starting transfers between devices, send(): return lax.ppermute(value, AXES, pairs)  39.2 us
    ppermute x16, waiting for transfers between devices, send(): return lax.ppermute(value, AXES, pairs)  35.7 us
    pallas_call x3, Pallas kernels, input_products(): pl.pallas_call(functools.partial(input_kernel, first, last), grid_spec=pl...  27.5 us
    pallas_call x3, Pallas kernels, weight_products(): pl.pallas_call(weight_kernel, grid_spec=grid_spec, out_shape=[jax.ShapeDt...  25.1 us
    all_gather x1, waiting for transfers between devices, per_device(): lax.all_gather(tie(jnp.maximum(jnp.maximum(peak_a, peak_b), peak_c), begu...  14.5 us
    unnamed x59, local copies, waits for them, and re-layouts  14.3 us
    all_gather x1, waiting for transfers between devices, per_device(): g_all = lax.all_gather(g, 'tensor', axis=0)  11 us
  transfers between devices with their start and end apart: 18, of which 9 were waited for; matrix products, arithmetic and copies ran while one was open for 9% of the time, Pallas kernels for 26%

profile of v3, /device:TPU:0, one launch (start us, length us, event | category | flops | bytes accessed | tf_op | source)
XLA Modules:
  0.0 201.5 jit_solution(11823541275585754175)
XLA Ops:
  7.2 0.7 all-gather.5.cloned.1.call-update
  8.0 1.7 collective-permute-start
  9.7 0.7 dynamic-slice_bitcast_fusion.order
  10.4 6.5 %weight_products.3 = (bf16[4,768,384]{2,1,0:T(8,128)(2,1)S(1)}, f32[8,384]{1,0:T(8,128)S(1)}) custom-call(s32[48]{0:T(128)S(1)} %dynamic-slice_bitcast_fusion.order, bf16[1024,6144]{1,0:T(8,128)(2,1)} %x_ref.5, bf16[1024,768]{1,0:T(8,128)(2,1)S(1)} %copy-done.6), custom_call_target="tpu_custom_call" | custom-call | flops 2415919104 | bytes 5505024 | tf_op jit(solution)/shard_map/weight_products/pallas_call | solution.py:102
  17.5 1.4 copy-done.19
  18.9 0.8 copy-done.22
  19.7 11.7 %collective-permute-start.3 = (bf16[384,768]{1,0:T(8,128)(2,1)}, bf16[384,768]{1,0:T(8,128)(2,1)S(1)}, u32[]{:S(2)}, u32[]{:S(2)}) collective-permute-start(bf16[384,768]{1,0:T(8,128)(2,1)} %tie.6), channel_id=1, source_target_pairs={{0,64},{1,17},{2,66},{3,19},{4,68},{5,21},{6,70},{7,23},{8,72},{9,... | collective-permute-start | bytes 1769480 | tf_op jit(solution)/shard_map/ppermute | solution.py:44
  31.3 3.2 %collective-permute-start.2 = (bf16[384,768]{1,0:T(8,128)(2,1)}, bf16[384,768]{1,0:T(8,128)(2,1)S(1)}, u32[]{:S(2)}, u32[]{:S(2)}) collective-permute-start(bf16[384,768]{1,0:T(8,128)(2,1)} %tie.6), channel_id=1, source_target_pairs={{0,96},{1,25},{2,98},{3,27},{4,100},{5,29},{6,102},{7,31},{8,104},... | collective-permute-start | bytes 1769480 | tf_op jit(solution)/shard_map/ppermute | solution.py:44
  34.6 11.0 %weight_products.4 = (bf16[4,768,384]{2,1,0:T(8,128)(2,1)S(1)}, bf16[4,768,384]{2,1,0:T(8,128)(2,1)S(1)}, f32[8,384]{1,0:T(8,128)S(1)}) custom-call(s32[48]{0:T(128)S(1)} %dynamic-slice_bitcast_fusion.order, bf16[1024,6144]{1,0:T(8,128)(2,1)} %x_ref.5, bf16[1024,768]{1,0:T(8,128)(2,1)S(1)} %copy-done.6), custom_call_target="tpu_custom_call" | custom-call | flops 4831838208 | bytes 11010048 | tf_op jit(solution)/shard_map/weight_products/pallas_call | solution.py:102
  45.6 1.5 copy-done.12
  47.1 1.4 copy-done.14
  48.5 0.6 copy-done.17
  49.1 0.8 copy-done.24
  50.4 2.9 %pad_maximum_fusion.refs_0_ = bf16[4,384,768]{2,1,0:T(8,128)(2,1)} fusion(bf16[1,384,768]{2,1,0:T(8,128)(2,1)} %bitcast.23, bf16[1,384,768]{2,1,0:T(8,128)(2,1)S(1)} %bitcast.25, bf16[1,384,768]{2,1,0:T(8,128)(2,1)S(1)} %bitcast.24, bf16[1,384,768]{2,1,0:T(8,128)(2,1)S(1)} %bitcast.22), kind=kLoop, calls=%fused_computation | loop fusion | flops 3538944 | bytes 4718592 | tf_op jit(solution)/shard_map/stack | solution.py:250
  53.2 2.9 %collective-permute-start.4 = (bf16[4,384,768]{2,1,0:T(8,128)(2,1)}, bf16[4,384,768]{2,1,0:T(8,128)(2,1)S(1)}, u32[]{:S(2)}, u32[]{:S(2)}) collective-permute-start(bf16[4,384,768]{2,1,0:T(8,128)(2,1)} %pad_maximum_fusion.refs_0_), channel_id=1, source_target_pairs={{0,8},{1,33},{2,10},{3,35},{4,12},{5,37},{6,14},{7,39},{8,16},{9,4... | collective-permute-start | bytes 7077896 | tf_op jit(solution)/shard_map/ppermute | solution.py:44
  56.1 4.1 %collective-permute-start.6 = (bf16[4,384,768]{2,1,0:T(8,128)(2,1)}, bf16[4,384,768]{2,1,0:T(8,128)(2,1)}, u32[]{:S(2)}, u32[]{:S(2)}) collective-permute-start(bf16[4,384,768]{2,1,0:T(8,128)(2,1)} %pad_maximum_fusion.refs_0_), channel_id=1, source_target_pairs={{0,24},{1,97},{2,26},{3,99},{4,28},{5,101},{6,30},{7,103},{8,0},{9... | collective-permute-start | bytes 7077896 | tf_op jit(solution)/shard_map/ppermute | solution.py:44
  60.2 7.6 %weight_products.5 = (bf16[4,768,384]{2,1,0:T(8,128)(2,1)}, f32[8,384]{1,0:T(8,128)S(1)}) custom-call(s32[48]{0:T(128)S(1)} %dynamic-slice_bitcast_fusion.order, bf16[1024,6144]{1,0:T(8,128)(2,1)} %x_ref.5, bf16[1024,768]{1,0:T(8,128)(2,1)S(1)} %copy-done.7), custom_call_target="tpu_custom_call" | custom-call | flops 2415919104 | bytes 5505024 | tf_op jit(solution)/shard_map/weight_products/pallas_call | solution.py:102
  67.8 3.1 %collective-permute-start.8 = (bf16[4,768,384]{2,1,0:T(8,128)(2,1)}, bf16[4,768,384]{2,1,0:T(8,128)(2,1)}, u32[]{:S(2)}, u32[]{:S(2)}) collective-permute-start(bf16[4,768,384]{2,1,0:T(8,128)(2,1)} %get-tuple-element.13), channel_id=1, source_target_pairs={{0,96},{1,25},{2,98},{3,27},{4,100},{5,29},{6,102},{7,31},{8,104},... | collective-permute-start | bytes 7077896 | tf_op jit(solution)/shard_map/ppermute | solution.py:44
  71.0 0.6 maximum_maximum_fusion.refs_0_
  71.6 11.0 %all-gather.5.cloned.1.call-done = bf16[8192,768]{1,0:T(8,128)(2,1)} async-done(((bf16[1024,768]{1,0:T(8,128)(2,1)}), bf16[8192,768]{1,0:T(8,128)(2,1)}) %all-gather.5.cloned.1.call-update) | async-done | bytes 12582928 | tf_op jit(solution)/shard_map/all_gather | solution.py:248
  82.6 7.1 %input_products.3.refs_2_.refs_1_ = f32[2,1024,384]{2,1,0:T(8,128)S(1)} custom-call(s32[48]{0:T(128)S(1)} %dynamic-slice_bitcast_fusion.order, bf16[8,1024,768]{2,1,0:T(8,128)(2,1)} %bitcast.18, bf16[4,384,768]{2,1,0:T(8,128)(2,1)} %pad_maximum_fusion.refs_0_), custom_call_target="tpu_custom_call" | custom-call | flops 2415919104 | bytes 8650752 | tf_op jit(solution)/shard_map/input_products/pallas_call | solution.py:199
  89.7 1.6 copy-done.2
  91.5 13.8 %collective-permute-done.6.refs_1_.refs_2_ = bf16[4,384,768]{2,1,0:T(8,128)(2,1)} collective-permute-done((bf16[4,384,768]{2,1,0:T(8,128)(2,1)}, bf16[4,384,768]{2,1,0:T(8,128)(2,1)}, u32[]{:S(2)}, u32[]{:S(2)}) %collective-permute-start.6) | collective-permute-done | bytes 2359328 | tf_op jit(solution)/shard_map/ppermute | solution.py:44
  105.3 5.4 %collective-permute-done.8 = bf16[4,768,384]{2,1,0:T(8,128)(2,1)} collective-permute-done((bf16[4,768,384]{2,1,0:T(8,128)(2,1)}, bf16[4,768,384]{2,1,0:T(8,128)(2,1)}, u32[]{:S(2)}, u32[]{:S(2)}) %collective-permute-start.8) | collective-permute-done | bytes 2359328 | tf_op jit(solution)/shard_map/ppermute | solution.py:44
  110.6 3.6 %add_convert_fusion.1 = (bf16[2,768,384]{2,1,0:T(8,128)(2,1)S(1)}, bf16[2,768,384]{2,1,0:T(8,128)(2,1)}) fusion(bf16[4,768,384]{2,1,0:T(8,128)(2,1)} %tie.8, bf16[4,768,384]{2,1,0:T(8,128)(2,1)S(1)} %copy-done.13, bf16[4,768,384]{2,1,0:T(8,128)(2,1)} %collective-permute-done.8), kind=kLoop, calls=%fused_computation.2 | loop fusion | flops 4718592 | bytes 7077888 | tf_op jit(solution)/shard_map/convert_element_type | solution.py:259
  114.2 1.7 collective-permute-start.10
  116.0 1.3 collective-permute-start.5
  117.3 1.3 slice.141
  118.7 2.3 %collective-permute-start.7 = (bf16[2,384,768]{2,1,0:T(8,128)(2,1)S(1)}, bf16[2,384,768]{2,1,0:T(8,128)(2,1)S(1)}, u32[]{:S(2)}, u32[]{:S(2)}) collective-permute-start(bf16[2,384,768]{2,1,0:T(8,128)(2,1)S(1)} %slice.141), channel_id=1, source_target_pairs={{0,24},{1,97},{2,26},{3,99},{4,28},{5,101},{6,30},{7,103},{8,0},{9... | collective-permute-start | bytes 3538952 | tf_op jit(solution)/shard_map/ppermute | solution.py:44
  121.0 1.5 collective-permute-start.11
  122.5 12.3 %input_products.4.refs_2_.refs_1_ = f32[2,1024,384]{2,1,0:T(8,128)S(1)} custom-call(s32[48]{0:T(128)S(1)} %dynamic-slice_bitcast_fusion.order, bf16[8,1024,768]{2,1,0:T(8,128)(2,1)} %bitcast.19, bf16[4,384,768]{2,1,0:T(8,128)(2,1)S(1)} %copy-done.5, bf16[4,384,768]{2,1,0:T(8,128)(2,1)} %collective-permute-done.6.refs_1_.refs_2_, f32[2,1024,384]{2,1,0:T(8,128)S(1)} %copy-done.3), custom_call_target="tpu_custom_call" | custom-call | flops 4831838208 | bytes 17301504 | tf_op jit(solution)/shard_map/input_products/pallas_call | solution.py:199
  134.8 1.6 copy-done
  136.5 5.6 %collective-permute-done.10.refs_0_ = bf16[2,768,384]{2,1,0:T(8,128)(2,1)S(1)} collective-permute-done((bf16[2,768,384]{2,1,0:T(8,128)(2,1)S(1)}, bf16[2,768,384]{2,1,0:T(8,128)(2,1)S(1)}, u32[]{:S(2)}, u32[]{:S(2)}) %collective-permute-start.10) | collective-permute-done | bytes 1179680 | tf_op jit(solution)/shard_map/ppermute | solution.py:44
  142.0 3.5 %collective-permute-done.5.refs_0_.refs_2_ = bf16[2,384,768]{2,1,0:T(8,128)(2,1)S(1)} collective-permute-done((bf16[2,384,768]{2,1,0:T(8,128)(2,1)S(1)}, bf16[2,384,768]{2,1,0:T(8,128)(2,1)S(1)}, u32[]{:S(2)}, u32[]{:S(2)}) %collective-permute-start.5) | collective-permute-done | bytes 1179680 | tf_op jit(solution)/shard_map/ppermute | solution.py:44
  145.6 1.0 copy-done.8
  146.6 1.0 copy-done.10
  147.8 4.0 %add_convert_fusion.5 = (bf16[1,768,384]{2,1,0:T(8,128)(2,1)S(1)}, bf16[1,768,384]{2,1,0:T(8,128)(2,1)S(1)}, bf16[1,768,384]{2,1,0:T(8,128)(2,1)S(1)}, bf16[1,768,384]{2,1,0:T(8,128)(2,1)S(1)}) fusion(bf16[2,768,384]{2,1,0:T(8,128)(2,1)} %tie.9, bf16[4,768,384]{2,1,0:T(8,128)(2,1)} %collective-permute-done.8, bf16[4,768,384]{2,1,0:T(8,128)(2,1)} %copy-done.14, ...), kind=kLoop, calls=%fused_computation.8 | loop fusion | flops 7077888 | bytes 9437184 | tf_op jit(solution)/shard_map/convert_element_type | solution.py:265
  152.0 2.2 %collective-permute-start.12 = (bf16[2,384,384]{2,1,0:T(8,128)(2,1)S(1)}, bf16[2,384,384]{2,1,0:T(8,128)(2,1)S(1)}, u32[]{:S(2)}, u32[]{:S(2)}) collective-permute-start(bf16[2,384,384]{2,1,0:T(8,128)(2,1)S(1)} %pad_maximum_fusion.1), channel_id=1, source_target_pairs={{0,24},{1,97},{2,26},{3,99},{4,28},{5,101},{6,30},{7,103},{8,0},{9... | collective-permute-start | bytes 1769480 | tf_op jit(solution)/shard_map/ppermute | solution.py:44
  154.4 8.1 %input_products.5.refs_1_ = bf16[1024,768]{1,0:T(8,128)(2,1)} custom-call(s32[48]{0:T(128)S(1)} %dynamic-slice_bitcast_fusion.order, bf16[8,1024,768]{2,1,0:T(8,128)(2,1)} %bitcast.20, bf16[2,384,768]{2,1,0:T(8,128)(2,1)S(1)} %copy-done.9, bf16[2,384,768]{2,1,0:T(8,128)(2,1)S(1)} %copy-done.11, f32[2,1024,384]{2,1,0:T(8,128)S(1)} %copy-done.1), custom_call_target="tpu_custom_call" | custom-call | flops 2415919104 | bytes 8650752 | tf_op jit(solution)/shard_map/input_products/pallas_call | solution.py:199
  162.5 0.9 fusion.2
  163.4 3.2 %collective-permute-start.15 = (bf16[384,384]{1,0:T(8,128)(2,1)}, bf16[384,384]{1,0:T(8,128)(2,1)}, u32[]{:S(2)}, u32[]{:S(2)}) collective-permute-start(bf16[384,384]{1,0:T(8,128)(2,1)} %fusion.2), channel_id=1, source_target_pairs={{0,24},{1,97},{2,26},{3,99},{4,28},{5,101},{6,30},{7,103},{8,0},{9... | collective-permute-start | bytes 884744 | tf_op jit(solution)/shard_map/ppermute | solution.py:44
  166.6 14.5 %all-gather.7.cloned.1.call-done = f32[1024,384]{1,0:T(8,128)} async-done(((f32[8,384]{1,0:T(8,128)}), f32[1024,384]{1,0:T(8,128)}) %all-gather.7.cloned.1.call-update) | async-done | bytes 1572880 | tf_op jit(solution)/shard_map/all_gather | solution.py:255
  181.1 1.9 fusion.1
  183.2 1.0 reduce_max.9
  184.2 7.1 %collective-permute-done.14 = bf16[384,384]{1,0:T(8,128)(2,1)} collective-permute-done((bf16[384,384]{1,0:T(8,128)(2,1)}, bf16[384,384]{1,0:T(8,128)(2,1)}, u32[]{:S(2)}, u32[]{:S(2)}) %collective-permute-start.14) | collective-permute-done | bytes 294944 | tf_op jit(solution)/shard_map/ppermute | solution.py:44
  191.2 1.3 bitcast_add_fusion.1
  192.5 0.7 fusion
  193.3 1.4 copy.13
  (78 shorter events, 2.2 us)
Async XLA Ops:
  7.2 3.2 %copy-start.6 = (bf16[1024,768]{1,0:T(8,128)(2,1)S(1)}, bf16[1024,768]{1,0:T(8,128)(2,1)}, u32[]{:S(2)}) copy-start(bf16[1024,768]{1,0:T(8,128)(2,1)} %g_ref.5) | copy-start | bytes 4718596
  7.2 75.4 %all-gather.5.cloned.1.call-start = ((), (), s32[]{:S(2)}) async-start(), calls=%async_computation | async-start | bytes 14155776 | tf_op jit(solution)/shard_map/all_gather | solution.py:248
  7.9 173.1 %all-gather.7.cloned.1.call-start = ((), (), s32[]{:S(2)}) async-start(), calls=%async_computation.1 | async-start | bytes 1585152 | tf_op jit(solution)/shard_map/all_gather | solution.py:255
  8.0 10.9 %collective-permute-start = (bf16[384,768]{1,0:T(8,128)(2,1)}, bf16[384,768]{1,0:T(8,128)(2,1)S(1)}, u32[]{:S(2)}, u32[]{:S(2)}) collective-permute-start(bf16[384,768]{1,0:T(8,128)(2,1)} %param.6), channel_id=1, source_target_pairs={{0,0},{1,16},{2,32},{3,48},{4,64},{5,80},{6,96},{7,112},{8,8},{9,2... | collective-permute-start | bytes 1769480 | tf_op jit(solution)/shard_map/ppermute | solution.py:44
  16.9 0.6 copy-start.15
  17.5 1.4 copy-start.19
  18.9 0.8 copy-start.22
  19.7 29.4 %collective-permute-start.3 = (bf16[384,768]{1,0:T(8,128)(2,1)}, bf16[384,768]{1,0:T(8,128)(2,1)S(1)}, u32[]{:S(2)}, u32[]{:S(2)}) collective-permute-start(bf16[384,768]{1,0:T(8,128)(2,1)} %tie.6), channel_id=1, source_target_pairs={{0,64},{1,17},{2,66},{3,19},{4,68},{5,21},{6,70},{7,23},{8,72},{9,... | collective-permute-start | bytes 1769480 | tf_op jit(solution)/shard_map/ppermute | solution.py:44
  31.3 18.6 %collective-permute-start.1 = (bf16[384,768]{1,0:T(8,128)(2,1)}, bf16[384,768]{1,0:T(8,128)(2,1)S(1)}, u32[]{:S(2)}, u32[]{:S(2)}) collective-permute-start(bf16[384,768]{1,0:T(8,128)(2,1)} %tie.6), channel_id=1, source_target_pairs={{0,32},{1,9},{2,34},{3,11},{4,36},{5,13},{6,38},{7,15},{8,40},{9,1... | collective-permute-start | bytes 1769480 | tf_op jit(solution)/shard_map/ppermute | solution.py:44
  31.3 18.6 %collective-permute-start.2 = (bf16[384,768]{1,0:T(8,128)(2,1)}, bf16[384,768]{1,0:T(8,128)(2,1)S(1)}, u32[]{:S(2)}, u32[]{:S(2)}) collective-permute-start(bf16[384,768]{1,0:T(8,128)(2,1)} %tie.6), channel_id=1, source_target_pairs={{0,96},{1,25},{2,98},{3,27},{4,100},{5,29},{6,102},{7,31},{8,104},... | collective-permute-start | bytes 1769480 | tf_op jit(solution)/shard_map/ppermute | solution.py:44
  34.6 56.8 %collective-permute-start.9 = (bf16[4,768,384]{2,1,0:T(8,128)(2,1)}, bf16[4,768,384]{2,1,0:T(8,128)(2,1)}, u32[]{:S(2)}, u32[]{:S(2)}) collective-permute-start(bf16[4,768,384]{2,1,0:T(8,128)(2,1)} %copy-done.19), channel_id=1, source_target_pairs={{0,32},{1,9},{2,34},{3,11},{4,36},{5,13},{6,38},{7,15},{8,40},{9,1... | collective-permute-start | bytes 7077896 | tf_op jit(solution)/shard_map/ppermute | solution.py:44
  45.6 1.5 copy-start.12
  47.1 1.4 copy-start.14
  48.5 0.6 copy-start.17
  49.1 1.3 copy-start.23
  49.1 0.8 copy-start.24
  50.4 9.9 %copy-start.7 = (bf16[1024,768]{1,0:T(8,128)(2,1)S(1)}, bf16[1024,768]{1,0:T(8,128)(2,1)}, u32[]{:S(2)}) copy-start(bf16[1024,768]{1,0:T(8,128)(2,1)} %g_ref.5) | copy-start | bytes 4718596
  53.2 17.7 %copy-start.16 = (f32[8,384]{1,0:T(8,128)S(1)}, f32[8,384]{1,0:T(8,128)}, u32[]{:S(2)}) copy-start(f32[8,384]{1,0:T(8,128)} %copy-done.15) | copy-start | bytes 36868
  53.2 17.7 %copy-start.18 = (f32[8,384]{1,0:T(8,128)S(1)}, f32[8,384]{1,0:T(8,128)}, u32[]{:S(2)}) copy-start(f32[8,384]{1,0:T(8,128)} %copy-done.17) | copy-start | bytes 36868
  53.2 38.2 %collective-permute-start.4 = (bf16[4,384,768]{2,1,0:T(8,128)(2,1)}, bf16[4,384,768]{2,1,0:T(8,128)(2,1)S(1)}, u32[]{:S(2)}, u32[]{:S(2)}) collective-permute-start(bf16[4,384,768]{2,1,0:T(8,128)(2,1)} %pad_maximum_fusion.refs_0_), channel_id=1, source_target_pairs={{0,8},{1,33},{2,10},{3,35},{4,12},{5,37},{6,14},{7,39},{8,16},{9,4... | collective-permute-start | bytes 7077896 | tf_op jit(solution)/shard_map/ppermute | solution.py:44
  56.1 49.1 %collective-permute-start.6 = (bf16[4,384,768]{2,1,0:T(8,128)(2,1)}, bf16[4,384,768]{2,1,0:T(8,128)(2,1)}, u32[]{:S(2)}, u32[]{:S(2)}) collective-permute-start(bf16[4,384,768]{2,1,0:T(8,128)(2,1)} %pad_maximum_fusion.refs_0_), channel_id=1, source_target_pairs={{0,24},{1,97},{2,26},{3,99},{4,28},{5,101},{6,30},{7,103},{8,0},{9... | collective-permute-start | bytes 7077896 | tf_op jit(solution)/shard_map/ppermute | solution.py:44
  67.8 42.8 %collective-permute-start.8 = (bf16[4,768,384]{2,1,0:T(8,128)(2,1)}, bf16[4,768,384]{2,1,0:T(8,128)(2,1)}, u32[]{:S(2)}, u32[]{:S(2)}) collective-permute-start(bf16[4,768,384]{2,1,0:T(8,128)(2,1)} %get-tuple-element.13), channel_id=1, source_target_pairs={{0,96},{1,25},{2,98},{3,27},{4,100},{5,29},{6,102},{7,31},{8,104},... | collective-permute-start | bytes 7077896 | tf_op jit(solution)/shard_map/ppermute | solution.py:44
  89.7 1.6 copy-start.2
  91.5 13.8 %copy-start.4 = (bf16[4,384,768]{2,1,0:T(8,128)(2,1)}, bf16[4,384,768]{2,1,0:T(8,128)(2,1)S(1)}, u32[]{:S(2)}) copy-start(bf16[4,384,768]{2,1,0:T(8,128)(2,1)S(1)} %collective-permute-done.4.refs_0_.refs_1_) | copy-start | bytes 7077892
  105.2 5.4 %copy-start.13 = (bf16[4,768,384]{2,1,0:T(8,128)(2,1)S(1)}, bf16[4,768,384]{2,1,0:T(8,128)(2,1)}, u32[]{:S(2)}) copy-start(bf16[4,768,384]{2,1,0:T(8,128)(2,1)} %copy-done.12) | copy-start | bytes 7077892
  110.6 5.3 %copy-start.5 = (bf16[4,384,768]{2,1,0:T(8,128)(2,1)S(1)}, bf16[4,384,768]{2,1,0:T(8,128)(2,1)}, u32[]{:S(2)}) copy-start(bf16[4,384,768]{2,1,0:T(8,128)(2,1)} %copy-done.4) | copy-start | bytes 7077892
  114.2 27.8 %collective-permute-start.10 = (bf16[2,768,384]{2,1,0:T(8,128)(2,1)S(1)}, bf16[2,768,384]{2,1,0:T(8,128)(2,1)S(1)}, u32[]{:S(2)}, u32[]{:S(2)}) collective-permute-start(bf16[2,768,384]{2,1,0:T(8,128)(2,1)S(1)} %get-tuple-element.26), channel_id=1, source_target_pairs={{0,32},{1,9},{2,34},{3,11},{4,36},{5,13},{6,38},{7,15},{8,40},{9,1... | collective-permute-start | bytes 3538952 | tf_op jit(solution)/shard_map/ppermute | solution.py:44
  115.9 6.6 %copy-start.3 = (f32[2,1024,384]{2,1,0:T(8,128)S(1)}, f32[2,1024,384]{2,1,0:T(8,128)}, u32[]{:S(2)}) copy-start(f32[2,1024,384]{2,1,0:T(8,128)} %copy-done.2) | copy-start | bytes 9437188
  116.0 29.5 %collective-permute-start.5 = (bf16[2,384,768]{2,1,0:T(8,128)(2,1)S(1)}, bf16[2,384,768]{2,1,0:T(8,128)(2,1)S(1)}, u32[]{:S(2)}, u32[]{:S(2)}) collective-permute-start(bf16[2,384,768]{2,1,0:T(8,128)(2,1)S(1)} %slice.140), channel_id=1, source_target_pairs={{0,8},{1,33},{2,10},{3,35},{4,12},{5,37},{6,14},{7,39},{8,16},{9,4... | collective-permute-start | bytes 3538952 | tf_op jit(solution)/shard_map/ppermute | solution.py:44
  118.7 26.9 %collective-permute-start.7 = (bf16[2,384,768]{2,1,0:T(8,128)(2,1)S(1)}, bf16[2,384,768]{2,1,0:T(8,128)(2,1)S(1)}, u32[]{:S(2)}, u32[]{:S(2)}) collective-permute-start(bf16[2,384,768]{2,1,0:T(8,128)(2,1)S(1)} %slice.141), channel_id=1, source_target_pairs={{0,24},{1,97},{2,26},{3,99},{4,28},{5,101},{6,30},{7,103},{8,0},{9... | collective-permute-start | bytes 3538952 | tf_op jit(solution)/shard_map/ppermute | solution.py:44
  121.0 26.9 %collective-permute-start.11 = (bf16[2,768,384]{2,1,0:T(8,128)(2,1)}, bf16[2,768,384]{2,1,0:T(8,128)(2,1)}, u32[]{:S(2)}, u32[]{:S(2)}) collective-permute-start(bf16[2,768,384]{2,1,0:T(8,128)(2,1)} %get-tuple-element.27), channel_id=1, source_target_pairs={{0,96},{1,25},{2,98},{3,27},{4,100},{5,29},{6,102},{7,31},{8,104},... | collective-permute-start | bytes 3538952 | tf_op jit(solution)/shard_map/ppermute | solution.py:44
  134.8 1.6 copy-start
  142.0 3.5 %copy-start.21 = (bf16[2,768,384]{2,1,0:T(8,128)(2,1)}, bf16[2,768,384]{2,1,0:T(8,128)(2,1)S(1)}, u32[]{:S(2)}) copy-start(bf16[2,768,384]{2,1,0:T(8,128)(2,1)S(1)} %collective-permute-done.10.refs_0_) | copy-start | bytes 3538948
  145.6 1.0 copy-start.8
  146.6 1.0 copy-start.10
  147.8 6.5 %copy-start.11 = (bf16[2,384,768]{2,1,0:T(8,128)(2,1)S(1)}, bf16[2,384,768]{2,1,0:T(8,128)(2,1)}, u32[]{:S(2)}) copy-start(bf16[2,384,768]{2,1,0:T(8,128)(2,1)} %copy-done.10) | copy-start | bytes 3538948
  151.8 2.6 %copy-start.9 = (bf16[2,384,768]{2,1,0:T(8,128)(2,1)S(1)}, bf16[2,384,768]{2,1,0:T(8,128)(2,1)}, u32[]{:S(2)}) copy-start(bf16[2,384,768]{2,1,0:T(8,128)(2,1)} %copy-done.8) | copy-start | bytes 3538948
  151.9 2.5 %copy-start.1 = (f32[2,1024,384]{2,1,0:T(8,128)S(1)}, f32[2,1024,384]{2,1,0:T(8,128)}, u32[]{:S(2)}) copy-start(f32[2,1024,384]{2,1,0:T(8,128)} %copy-done) | copy-start | bytes 9437188
  152.0 10.5 %collective-permute-start.12 = (bf16[2,384,384]{2,1,0:T(8,128)(2,1)S(1)}, bf16[2,384,384]{2,1,0:T(8,128)(2,1)S(1)}, u32[]{:S(2)}, u32[]{:S(2)}) collective-permute-start(bf16[2,384,384]{2,1,0:T(8,128)(2,1)S(1)} %pad_maximum_fusion.1), channel_id=1, source_target_pairs={{0,24},{1,97},{2,26},{3,99},{4,28},{5,101},{6,30},{7,103},{8,0},{9... | collective-permute-start | bytes 1769480 | tf_op jit(solution)/shard_map/ppermute | solution.py:44
  154.3 12.3 %collective-permute-start.13 = (bf16[2,384,384]{2,1,0:T(8,128)(2,1)S(1)}, bf16[2,384,384]{2,1,0:T(8,128)(2,1)S(1)}, u32[]{:S(2)}, u32[]{:S(2)}) collective-permute-start(bf16[2,384,384]{2,1,0:T(8,128)(2,1)S(1)} %pad_maximum_fusion.2), channel_id=1, source_target_pairs={{0,8},{1,33},{2,10},{3,35},{4,12},{5,37},{6,14},{7,39},{8,16},{9,4... | collective-permute-start | bytes 1769480 | tf_op jit(solution)/shard_map/ppermute | solution.py:44
  162.5 18.5 %copy-start.27 = (bf16[2,384,384]{2,1,0:T(8,128)(2,1)}, bf16[2,384,384]{2,1,0:T(8,128)(2,1)S(1)}, u32[]{:S(2)}) copy-start(bf16[2,384,384]{2,1,0:T(8,128)(2,1)S(1)} %collective-permute-done.12) | copy-start | bytes 1769476
  163.4 20.8 %collective-permute-start.15 = (bf16[384,384]{1,0:T(8,128)(2,1)}, bf16[384,384]{1,0:T(8,128)(2,1)}, u32[]{:S(2)}, u32[]{:S(2)}) collective-permute-start(bf16[384,384]{1,0:T(8,128)(2,1)} %fusion.2), channel_id=1, source_target_pairs={{0,24},{1,97},{2,26},{3,99},{4,28},{5,101},{6,30},{7,103},{8,0},{9... | collective-permute-start | bytes 884744 | tf_op jit(solution)/shard_map/ppermute | solution.py:44
  166.6 14.5 %copy-start.25 = (bf16[2,384,384]{2,1,0:T(8,128)(2,1)}, bf16[2,384,384]{2,1,0:T(8,128)(2,1)S(1)}, u32[]{:S(2)}) copy-start(bf16[2,384,384]{2,1,0:T(8,128)(2,1)S(1)} %collective-permute-done.13.refs_0_) | copy-start | bytes 1769476
  181.1 2.1 %copy-start.20 = (f32[1024,384]{1,0:T(8,128)S(1)}, f32[1024,384]{1,0:T(8,128)}, u32[]{:S(2)}) copy-start(f32[1024,384]{1,0:T(8,128)} %all-gather.7.cloned.1.call-done) | copy-start | bytes 4718596
  181.1 10.2 %copy-start.26 = (bf16[2,384,384]{2,1,0:T(8,128)(2,1)S(1)}, bf16[2,384,384]{2,1,0:T(8,128)(2,1)}, u32[]{:S(2)}) copy-start(bf16[2,384,384]{2,1,0:T(8,128)(2,1)} %tie.11) | copy-start | bytes 1769476
  183.0 8.3 %copy-start.28 = (bf16[2,384,384]{2,1,0:T(8,128)(2,1)S(1)}, bf16[2,384,384]{2,1,0:T(8,128)(2,1)}, u32[]{:S(2)}) copy-start(bf16[2,384,384]{2,1,0:T(8,128)(2,1)} %copy-done.27) | copy-start | bytes 1769476
  183.0 8.2 %collective-permute-start.14 = (bf16[384,384]{1,0:T(8,128)(2,1)}, bf16[384,384]{1,0:T(8,128)(2,1)}, u32[]{:S(2)}, u32[]{:S(2)}) collective-permute-start(bf16[384,384]{1,0:T(8,128)(2,1)} %fusion.1), channel_id=1, source_target_pairs={{0,8},{1,33},{2,10},{3,35},{4,12},{5,37},{6,14},{7,39},{8,16},{9,4... | collective-permute-start | bytes 884744 | tf_op jit(solution)/shard_map/ppermute | solution.py:44
Sparse Core Ops, SparseCore 0:
  9.7 72.8 all-gather.4
  105.4 75.6 all-gather.6

commit v4 on v2

--- a/solution.py
+++ b/solution.py
@@ -135,12 +135,15 @@
 W_BASE = 2 * BLOCKS
 
 
-def block_product(g_ref, w_refs, per_array):
-    n = pl.program_id(0)
-    w = w_refs[0][0]
-    for q in range(1, len(w_refs)):
-        w = jnp.where(n >= q * per_array, w_refs[q][0], w)
-    return lax.dot_general(g_ref[0], w, (((1,), (1,)), ((), ())), preferred_element_type=F32)
+def add_product(sum_ref, half, g_ref, w_refs, per_array):
+    n = pl.program_id(0)
+    for q, w_ref in enumerate(w_refs):
+
+        @pl.when(n // per_array == q)
+        def _(w_ref=w_ref):
+            sum_ref[half] += lax.dot_general(
+                g_ref[0], w_ref[0], (((1,), (1,)), ((), ())), preferred_element_type=F32
+            )
 
 
 def begin_kernel(order, g_ref, w0, w1, w2, sum_ref):
@@ -150,7 +153,7 @@
     def _():
         sum_ref[...] = jnp.zeros_like(sum_ref)
 
-    sum_ref[order[BLOCKS + n]] += block_product(g_ref, (w0, w1, w2), 4)
+    add_product(sum_ref, order[BLOCKS + n], g_ref, (w0, w1, w2), 4)
 
 
 def end_kernel(order, g_ref, w0, w1, begun_ref, out_ref, sum_ref):
@@ -160,7 +163,7 @@
     def _():
         sum_ref[...] = begun_ref[...]
 
-    sum_ref[order[BLOCKS + 12 + n]] += block_product(g_ref, (w0, w1), 2)
+    add_product(sum_ref, order[BLOCKS + 12 + n], g_ref, (w0, w1), 2)
 
     @pl.when(n == pl.num_programs(0) - 1)
     def _():
@@ -222,6 +225,25 @@
     )(value, *after)
 
 
+def halves_kernel(up_ref, down_ref, ahead_ref, back_ref):
+    ahead_ref[...] = up_ref[...]
+    back_ref[...] = down_ref[...]
+
+
+def far_halves(up, down):
+    block = (1,) + up.shape[1:]
+    half = jax.ShapeDtypeStruct((2,) + up.shape[1:], up.dtype)
+    return pl.pallas_call(
+        halves_kernel,
+        grid=(2,),
+        in_specs=[pl.BlockSpec(block, lambda n: (n, 0, 0)), pl.BlockSpec(block, lambda n: (n + 2, 0, 0))],
+        out_specs=[pl.BlockSpec(block, lambda n: (n, 0, 0))] * 2,
+        out_shape=[half, half],
+        cost_estimate=pl.CostEstimate(flops=1, bytes_accessed=1, transcendentals=0),
+        name="far_halves",
+    )(up, down)
+
+
 def per_device(x_in, g, w):
     dp = lax.axis_index("dp")
     t = lax.axis_index("tensor")
@@ -245,11 +267,12 @@
     peaks = lax.all_gather(jnp.maximum(jnp.maximum(peak_a, peak_b), peak_c), AXES)
     u = tie(u, up, down)
 
-    far = [send(up[:2], SECOND[1]), send(down[2:], SECOND[-1])]
+    ahead, back = far_halves(up, down)
+    far = [send(ahead, SECOND[1]), send(back, SECOND[-1])]
     r = send(add(low[0:2], u[0:2]).astype(BF16), FIRST[1])
     s = send(add(low[2:4], v[0:2]).astype(BF16), FIRST[-1])
     begun = input_products(order, g_all, [line, up, down])
-    r = tie(r, begun, *far)
+    r = tie(r, begun)
 
     e = [add(high[0], v[2], r[0]), add(high[1], v[3], r[1]), add(high[2], u[2], s[0]), add(high[3], u[3], s[1])]
     e = [b.astype(BF16) for b in e]

time: 188 us -> 204 us (1.085)
  the two profiles are of different devices: /device:TPU:16 before, /device:TPU:0 now
where the time goes in v4:
time: 204 us; the launch traced here: 201 us
  waiting for transfers between devices  63.8 us (31%)
  Pallas kernels  55.1 us (27%)
  starting transfers between devices  34.5 us (17%)
  other arithmetic  19.7 us (10%)
  between operations  14.2 us (7%)
  local copies, waits for them, and re-layouts  14.1 us (7%)
    ppermute x16, waiting for transfers between devices, send(): return lax.ppermute(value, AXES, pairs)  63.1 us
    ppermute x16, starting transfers between devices, send(): return lax.ppermute(value, AXES, pairs)  34.5 us
    pallas_call x2, Pallas kernels, input_products(): pl.pallas_call(begin_kernel if begun is None else end_kernel, grid_spec=p...  26.2 us
    pallas_call x3, Pallas kernels, weight_products(): pl.pallas_call(weight_kernel, grid_spec=grid_spec, out_shape=[jax.ShapeDt...  26.1 us
    unnamed x47, local copies, waits for them, and re-layouts  13.2 us
    convert_element_type x1, other arithmetic, per_device(): r = send(add(low[0:2], u[0:2]).astype(BF16), FIRST[1])  4.29 us
    convert_element_type x1, other arithmetic, per_device(): e = [b.astype(BF16) for b in e]  4.22 us
  transfers between devices with their start and end apart: 18, of which 7 were waited for; matrix products, arithmetic and copies ran while one was open for 9% of the time, Pallas kernels for 27%

profile of v4, /device:TPU:0, one launch (start us, length us, event | category | flops | bytes accessed | tf_op | source)
XLA Modules:
  0.0 201.4 jit_solution(5705031872893239862)
XLA Ops:
  7.2 0.7 all-gather.5.cloned.1.call-update
  8.0 1.7 collective-permute-start
  9.7 0.7 dynamic-slice_bitcast_fusion.order
  10.4 7.6 %weight_products.3 = (bf16[4,768,384]{2,1,0:T(8,128)(2,1)}, f32[8,384]{1,0:T(8,128)S(1)}) custom-call(s32[48]{0:T(128)S(1)} %dynamic-slice_bitcast_fusion.order, bf16[1024,6144]{1,0:T(8,128)(2,1)} %x_ref.5, bf16[1024,768]{1,0:T(8,128)(2,1)S(1)} %copy-done), custom_call_target="tpu_custom_call" | custom-call | flops 2415919104 | bytes 5505024 | tf_op jit(solution)/shard_map/weight_products/pallas_call | solution.py:100
  17.9 0.6 copy-done.8
  18.5 3.4 %collective-permute-start.9 = (bf16[4,768,384]{2,1,0:T(8,128)(2,1)}, bf16[4,768,384]{2,1,0:T(8,128)(2,1)}, u32[]{:S(2)}, u32[]{:S(2)}) collective-permute-start(bf16[4,768,384]{2,1,0:T(8,128)(2,1)} %get-tuple-element.19), channel_id=1, source_target_pairs={{0,32},{1,9},{2,34},{3,11},{4,36},{5,13},{6,38},{7,15},{8,40},{9,1... | collective-permute-start | bytes 7077896 | tf_op jit(solution)/shard_map/ppermute | solution.py:42
  21.9 0.8 copy-done.17
  22.7 8.7 %collective-permute-start.3 = (bf16[384,768]{1,0:T(8,128)(2,1)}, bf16[384,768]{1,0:T(8,128)(2,1)S(1)}, u32[]{:S(2)}, u32[]{:S(2)}) collective-permute-start(bf16[384,768]{1,0:T(8,128)(2,1)} %tie.5), channel_id=1, source_target_pairs={{0,64},{1,17},{2,66},{3,19},{4,68},{5,21},{6,70},{7,23},{8,72},{9,... | collective-permute-start | bytes 1769480 | tf_op jit(solution)/shard_map/ppermute | solution.py:42
  31.5 2.0 %collective-permute-start.1 = (bf16[384,768]{1,0:T(8,128)(2,1)}, bf16[384,768]{1,0:T(8,128)(2,1)S(1)}, u32[]{:S(2)}, u32[]{:S(2)}) collective-permute-start(bf16[384,768]{1,0:T(8,128)(2,1)} %tie.5), channel_id=1, source_target_pairs={{0,32},{1,9},{2,34},{3,11},{4,36},{5,13},{6,38},{7,15},{8,40},{9,1... | collective-permute-start | bytes 1769480 | tf_op jit(solution)/shard_map/ppermute | solution.py:42
  33.5 7.6 %weight_products.5 = (bf16[4,768,384]{2,1,0:T(8,128)(2,1)}, f32[8,384]{1,0:T(8,128)S(1)}) custom-call(s32[48]{0:T(128)S(1)} %dynamic-slice_bitcast_fusion.order, bf16[1024,6144]{1,0:T(8,128)(2,1)} %x_ref.5, bf16[1024,768]{1,0:T(8,128)(2,1)S(1)} %copy-done), custom_call_target="tpu_custom_call" | custom-call | flops 2415919104 | bytes 5505024 | tf_op jit(solution)/shard_map/weight_products/pallas_call | solution.py:100
  41.0 11.0 %weight_products.4 = (bf16[4,768,384]{2,1,0:T(8,128)(2,1)S(1)}, bf16[4,768,384]{2,1,0:T(8,128)(2,1)S(1)}, f32[8,384]{1,0:T(8,128)S(1)}) custom-call(s32[48]{0:T(128)S(1)} %dynamic-slice_bitcast_fusion.order, bf16[1024,6144]{1,0:T(8,128)(2,1)} %x_ref.5, bf16[1024,768]{1,0:T(8,128)(2,1)S(1)} %copy-done), custom_call_target="tpu_custom_call" | custom-call | flops 4831838208 | bytes 11010048 | tf_op jit(solution)/shard_map/weight_products/pallas_call | solution.py:100
  52.1 1.5 copy-done.5
  53.6 1.4 copy-done.6
  55.0 0.6 copy-done.10
  55.6 3.9 %collective-permute-done.3.refs_0_ = bf16[384,768]{1,0:T(8,128)(2,1)S(1)} collective-permute-done((bf16[384,768]{1,0:T(8,128)(2,1)}, bf16[384,768]{1,0:T(8,128)(2,1)S(1)}, u32[]{:S(2)}, u32[]{:S(2)}) %collective-permute-start.3) | collective-permute-done | bytes 589856 | tf_op jit(solution)/shard_map/ppermute | solution.py:42
  59.5 0.8 copy-done.19
  60.3 3.9 %collective-permute-done.1 = bf16[384,768]{1,0:T(8,128)(2,1)S(1)} collective-permute-done((bf16[384,768]{1,0:T(8,128)(2,1)}, bf16[384,768]{1,0:T(8,128)(2,1)S(1)}, u32[]{:S(2)}, u32[]{:S(2)}) %collective-permute-start.1) | collective-permute-done | bytes 589856 | tf_op jit(solution)/shard_map/ppermute | solution.py:42
  64.3 2.9 %pad_maximum_fusion.w0 = bf16[4,384,768]{2,1,0:T(8,128)(2,1)} fusion(bf16[1,384,768]{2,1,0:T(8,128)(2,1)} %bitcast.22, bf16[1,384,768]{2,1,0:T(8,128)(2,1)S(1)} %bitcast.23, bf16[1,384,768]{2,1,0:T(8,128)(2,1)S(1)} %bitcast.24, bf16[1,384,768]{2,1,0:T(8,128)(2,1)S(1)} %bitcast.21), kind=kLoop, calls=%fused_computation | loop fusion | flops 3538944 | bytes 4718592 | tf_op jit(solution)/shard_map/stack | solution.py:263
  67.1 1.9 collective-permute-start.4
  69.1 1.5 collective-permute-start.5
  70.6 2.1 %collective-permute-start.8 = (bf16[4,768,384]{2,1,0:T(8,128)(2,1)}, bf16[4,768,384]{2,1,0:T(8,128)(2,1)}, u32[]{:S(2)}, u32[]{:S(2)}) collective-permute-start(bf16[4,768,384]{2,1,0:T(8,128)(2,1)} %get-tuple-element.17), channel_id=1, source_target_pairs={{0,96},{1,25},{2,98},{3,27},{4,100},{5,29},{6,102},{7,31},{8,104},... | collective-permute-start | bytes 7077896 | tf_op jit(solution)/shard_map/ppermute | solution.py:42
  72.7 0.6 maximum_maximum_fusion
  73.3 24.3 %collective-permute-done.4.up_ref.w1.refs_1_ = bf16[4,384,768]{2,1,0:T(8,128)(2,1)S(1)} collective-permute-done((bf16[4,384,768]{2,1,0:T(8,128)(2,1)}, bf16[4,384,768]{2,1,0:T(8,128)(2,1)S(1)}, u32[]{:S(2)}, u32[]{:S(2)}) %collective-permute-start.4) | collective-permute-done | bytes 2359328 | tf_op jit(solution)/shard_map/ppermute | solution.py:42
  97.6 22.9 %collective-permute-done.5.down_ref.w2.refs_2_ = bf16[4,384,768]{2,1,0:T(8,128)(2,1)} collective-permute-done((bf16[4,384,768]{2,1,0:T(8,128)(2,1)}, bf16[4,384,768]{2,1,0:T(8,128)(2,1)}, u32[]{:S(2)}, u32[]{:S(2)}) %collective-permute-start.5) | collective-permute-done | bytes 2359328 | tf_op jit(solution)/shard_map/ppermute | solution.py:42
  120.5 4.5 %collective-permute-done.8 = bf16[4,768,384]{2,1,0:T(8,128)(2,1)} collective-permute-done((bf16[4,768,384]{2,1,0:T(8,128)(2,1)}, bf16[4,768,384]{2,1,0:T(8,128)(2,1)}, u32[]{:S(2)}, u32[]{:S(2)}) %collective-permute-start.8) | collective-permute-done | bytes 2359328 | tf_op jit(solution)/shard_map/ppermute | solution.py:42
  125.0 4.3 %add_convert_fusion.1 = (bf16[2,768,384]{2,1,0:T(8,128)(2,1)}, bf16[2,768,384]{2,1,0:T(8,128)(2,1)}) fusion(bf16[4,768,384]{2,1,0:T(8,128)(2,1)} %tie.7, bf16[4,768,384]{2,1,0:T(8,128)(2,1)} %copy-done.5, bf16[4,768,384]{2,1,0:T(8,128)(2,1)} %collective-permute-done.8), kind=kLoop, calls=%fused_computation.2 | loop fusion | flops 4718592 | bytes 7077888 | tf_op jit(solution)/shard_map/convert_element_type | solution.py:272
  129.3 3.7 %collective-permute-start.11 = (bf16[2,768,384]{2,1,0:T(8,128)(2,1)}, bf16[2,768,384]{2,1,0:T(8,128)(2,1)}, u32[]{:S(2)}, u32[]{:S(2)}) collective-permute-start(bf16[2,768,384]{2,1,0:T(8,128)(2,1)} %get-tuple-element.31), channel_id=1, source_target_pairs={{0,96},{1,25},{2,98},{3,27},{4,100},{5,29},{6,102},{7,31},{8,104},... | collective-permute-start | bytes 3538952 | tf_op jit(solution)/shard_map/ppermute | solution.py:42
  133.0 2.8 %far_halves.1 = (bf16[2,384,768]{2,1,0:T(8,128)(2,1)}, bf16[2,384,768]{2,1,0:T(8,128)(2,1)}) custom-call(bf16[4,384,768]{2,1,0:T(8,128)(2,1)} %copy-done.3, bf16[4,384,768]{2,1,0:T(8,128)(2,1)} %collective-permute-done.5.down_ref.w2.refs_2_), custom_call_target="tpu_custom_call" | custom-call | flops 1 | bytes 1 | tf_op jit(solution)/shard_map/far_halves/pallas_call | solution.py:236
  135.7 3.2 %collective-permute-start.7 = (bf16[2,384,768]{2,1,0:T(8,128)(2,1)}, bf16[2,384,768]{2,1,0:T(8,128)(2,1)}, u32[]{:S(2)}, u32[]{:S(2)}) collective-permute-start(bf16[2,384,768]{2,1,0:T(8,128)(2,1)} %get-tuple-element.15), channel_id=1, source_target_pairs={{0,24},{1,97},{2,26},{3,99},{4,28},{5,101},{6,30},{7,103},{8,0},{9... | collective-permute-start | bytes 3538952 | tf_op jit(solution)/shard_map/ppermute | solution.py:42
  139.0 17.8 %input_products.2.begun_ref.refs_1_ = f32[2,1024,384]{2,1,0:T(8,128)S(1)} custom-call(s32[48]{0:T(128)S(1)} %dynamic-slice_bitcast_fusion.order, bf16[8,1024,768]{2,1,0:T(8,128)(2,1)} %bitcast.18, bf16[4,384,768]{2,1,0:T(8,128)(2,1)} %pad_maximum_fusion.w0, bf16[4,384,768]{2,1,0:T(8,128)(2,1)S(1)} %copy-done.4, ...), custom_call_target="tpu_custom_call" | custom-call | flops 7247757312 | bytes 25952256 | tf_op jit(solution)/shard_map/input_products/pallas_call | solution.py:197
  156.8 1.7 copy-done.1
  158.5 1.7 copy-done.7
  160.2 4.2 %add_convert_fusion.5 = (bf16[1,768,384]{2,1,0:T(8,128)(2,1)}, bf16[1,768,384]{2,1,0:T(8,128)(2,1)S(1)}, bf16[1,768,384]{2,1,0:T(8,128)(2,1)S(1)}, bf16[1,768,384]{2,1,0:T(8,128)(2,1)S(1)}) fusion(bf16[2,768,384]{2,1,0:T(8,128)(2,1)} %tie.8, bf16[4,768,384]{2,1,0:T(8,128)(2,1)} %collective-permute-done.8, bf16[4,768,384]{2,1,0:T(8,128)(2,1)S(1)} %copy-done.7, ...), kind=kLoop, calls=%fused_computation.8 | loop fusion | flops 7077888 | bytes 9437184 | tf_op jit(solution)/shard_map/convert_element_type | solution.py:278
  164.6 0.6 copy-done.15
  165.5 0.9 pad_maximum_fusion.1
  166.4 3.0 %collective-permute-start.12 = (bf16[2,384,384]{2,1,0:T(8,128)(2,1)}, bf16[2,384,384]{2,1,0:T(8,128)(2,1)}, u32[]{:S(2)}, u32[]{:S(2)}) collective-permute-start(bf16[2,384,384]{2,1,0:T(8,128)(2,1)} %pad_maximum_fusion.1), channel_id=1, source_target_pairs={{0,24},{1,97},{2,26},{3,99},{4,28},{5,101},{6,30},{7,103},{8,0},{9... | collective-permute-start | bytes 1769480 | tf_op jit(solution)/shard_map/ppermute | solution.py:42
  169.4 8.4 %input_products.3.refs_1_ = bf16[1024,768]{1,0:T(8,128)(2,1)} custom-call(s32[48]{0:T(128)S(1)} %dynamic-slice_bitcast_fusion.order, bf16[8,1024,768]{2,1,0:T(8,128)(2,1)} %bitcast.19, bf16[2,384,768]{2,1,0:T(8,128)(2,1)S(1)} %collective-permute-done.6.w0, bf16[2,384,768]{2,1,0:T(8,128)(2,1)} %collective-permute-done.7.w1, f32[2,1024,384]{2,1,0:T(8,128)S(1)} %copy-done.2), custom_call_target="tpu_custom_call" | custom-call | flops 2415919104 | bytes 8650752 | tf_op jit(solution)/shard_map/input_products/pallas_call | solution.py:197
  177.8 0.8 copy-done.21
  178.6 1.1 copy-done.16
  179.7 1.9 fusion.1
  181.6 1.9 fusion.2
  183.4 3.1 %collective-permute-start.15 = (bf16[384,384]{1,0:T(8,128)(2,1)}, bf16[384,384]{1,0:T(8,128)(2,1)S(1)}, u32[]{:S(2)}, u32[]{:S(2)}) collective-permute-start(bf16[384,384]{1,0:T(8,128)(2,1)} %fusion.2), channel_id=1, source_target_pairs={{0,24},{1,97},{2,26},{3,99},{4,28},{5,101},{6,30},{7,103},{8,0},{9... | collective-permute-start | bytes 884744 | tf_op jit(solution)/shard_map/ppermute | solution.py:42
  186.6 1.0 reduce_max.9
  187.6 2.2 %collective-permute-done.14 = bf16[384,384]{1,0:T(8,128)(2,1)} collective-permute-done((bf16[384,384]{1,0:T(8,128)(2,1)}, bf16[384,384]{1,0:T(8,128)(2,1)}, u32[]{:S(2)}, u32[]{:S(2)}) %collective-permute-start.14) | collective-permute-done | bytes 294944 | tf_op jit(solution)/shard_map/ppermute | solution.py:42
  189.8 1.3 collective-permute-done.15
  191.1 1.3 bitcast_add_fusion.1
  192.4 0.7 fusion
  193.2 1.4 copy.12
  (63 shorter events, 0.6 us)
Async XLA Ops:
  7.2 3.2 %copy-start = (bf16[1024,768]{1,0:T(8,128)(2,1)S(1)}, bf16[1024,768]{1,0:T(8,128)(2,1)}, u32[]{:S(2)}) copy-start(bf16[1024,768]{1,0:T(8,128)(2,1)} %g_ref.5) | copy-start | bytes 4718596
  7.2 131.8 %all-gather.5.cloned.1.call-start = ((), (), s32[]{:S(2)}) async-start(), calls=%async_computation | async-start | bytes 14155776 | tf_op jit(solution)/shard_map/all_gather | solution.py:261
  7.9 169.9 %all-gather.7.cloned.1.call-start = ((), (), s32[]{:S(2)}) async-start(), calls=%async_computation.1 | async-start | bytes 1585152 | tf_op jit(solution)/shard_map/all_gather | solution.py:267
  8.0 13.9 %collective-permute-start = (bf16[384,768]{1,0:T(8,128)(2,1)}, bf16[384,768]{1,0:T(8,128)(2,1)S(1)}, u32[]{:S(2)}, u32[]{:S(2)}) collective-permute-start(bf16[384,768]{1,0:T(8,128)(2,1)} %param.6), channel_id=1, source_target_pairs={{0,0},{1,16},{2,32},{3,48},{4,64},{5,80},{6,96},{7,112},{8,8},{9,2... | collective-permute-start | bytes 1769480 | tf_op jit(solution)/shard_map/ppermute | solution.py:42
  17.9 0.6 copy-start.8
  18.5 54.8 %collective-permute-start.9 = (bf16[4,768,384]{2,1,0:T(8,128)(2,1)}, bf16[4,768,384]{2,1,0:T(8,128)(2,1)}, u32[]{:S(2)}, u32[]{:S(2)}) collective-permute-start(bf16[4,768,384]{2,1,0:T(8,128)(2,1)} %get-tuple-element.19), channel_id=1, source_target_pairs={{0,32},{1,9},{2,34},{3,11},{4,36},{5,13},{6,38},{7,15},{8,40},{9,1... | collective-permute-start | bytes 7077896 | tf_op jit(solution)/shard_map/ppermute | solution.py:42
  21.9 0.8 copy-start.17
  22.7 36.8 %collective-permute-start.3 = (bf16[384,768]{1,0:T(8,128)(2,1)}, bf16[384,768]{1,0:T(8,128)(2,1)S(1)}, u32[]{:S(2)}, u32[]{:S(2)}) collective-permute-start(bf16[384,768]{1,0:T(8,128)(2,1)} %tie.5), channel_id=1, source_target_pairs={{0,64},{1,17},{2,66},{3,19},{4,68},{5,21},{6,70},{7,23},{8,72},{9,... | collective-permute-start | bytes 1769480 | tf_op jit(solution)/shard_map/ppermute | solution.py:42
  31.4 28.9 %collective-permute-start.2 = (bf16[384,768]{1,0:T(8,128)(2,1)}, bf16[384,768]{1,0:T(8,128)(2,1)S(1)}, u32[]{:S(2)}, u32[]{:S(2)}) collective-permute-start(bf16[384,768]{1,0:T(8,128)(2,1)} %tie.5), channel_id=1, source_target_pairs={{0,96},{1,25},{2,98},{3,27},{4,100},{5,29},{6,102},{7,31},{8,104},... | collective-permute-start | bytes 1769480 | tf_op jit(solution)/shard_map/ppermute | solution.py:42
  31.5 32.8 %collective-permute-start.1 = (bf16[384,768]{1,0:T(8,128)(2,1)}, bf16[384,768]{1,0:T(8,128)(2,1)S(1)}, u32[]{:S(2)}, u32[]{:S(2)}) collective-permute-start(bf16[384,768]{1,0:T(8,128)(2,1)} %tie.5), channel_id=1, source_target_pairs={{0,32},{1,9},{2,34},{3,11},{4,36},{5,13},{6,38},{7,15},{8,40},{9,1... | collective-permute-start | bytes 1769480 | tf_op jit(solution)/shard_map/ppermute | solution.py:42
  52.1 1.5 copy-start.5
  53.6 1.4 copy-start.6
  55.0 0.6 copy-start.10
  55.6 8.7 %copy-start.18 = (bf16[384,768]{1,0:T(8,128)(2,1)S(1)}, bf16[384,768]{1,0:T(8,128)(2,1)}, u32[]{:S(2)}) copy-start(bf16[384,768]{1,0:T(8,128)(2,1)} %tie.5) | copy-start | bytes 1769476
  59.5 0.8 copy-start.19
  64.3 8.4 %copy-start.9 = (f32[8,384]{1,0:T(8,128)S(1)}, f32[8,384]{1,0:T(8,128)}, u32[]{:S(2)}) copy-start(f32[8,384]{1,0:T(8,128)} %copy-done.8) | copy-start | bytes 36868
  64.3 8.4 %copy-start.11 = (f32[8,384]{1,0:T(8,128)S(1)}, f32[8,384]{1,0:T(8,128)}, u32[]{:S(2)}) copy-start(f32[8,384]{1,0:T(8,128)} %copy-done.10) | copy-start | bytes 36868
  67.1 30.5 %collective-permute-start.4 = (bf16[4,384,768]{2,1,0:T(8,128)(2,1)}, bf16[4,384,768]{2,1,0:T(8,128)(2,1)S(1)}, u32[]{:S(2)}, u32[]{:S(2)}) collective-permute-start(bf16[4,384,768]{2,1,0:T(8,128)(2,1)} %pad_maximum_fusion.w0), channel_id=1, source_target_pairs={{0,8},{1,33},{2,10},{3,35},{4,12},{5,37},{6,14},{7,39},{8,16},{9,4... | collective-permute-start | bytes 7077896 | tf_op jit(solution)/shard_map/ppermute | solution.py:42
  69.1 51.5 %collective-permute-start.5 = (bf16[4,384,768]{2,1,0:T(8,128)(2,1)}, bf16[4,384,768]{2,1,0:T(8,128)(2,1)}, u32[]{:S(2)}, u32[]{:S(2)}) collective-permute-start(bf16[4,384,768]{2,1,0:T(8,128)(2,1)} %pad_maximum_fusion.w0), channel_id=1, source_target_pairs={{0,24},{1,97},{2,26},{3,99},{4,28},{5,101},{6,30},{7,103},{8,0},{9... | collective-permute-start | bytes 7077896 | tf_op jit(solution)/shard_map/ppermute | solution.py:42
  70.6 54.4 %collective-permute-start.8 = (bf16[4,768,384]{2,1,0:T(8,128)(2,1)}, bf16[4,768,384]{2,1,0:T(8,128)(2,1)}, u32[]{:S(2)}, u32[]{:S(2)}) collective-permute-start(bf16[4,768,384]{2,1,0:T(8,128)(2,1)} %get-tuple-element.17), channel_id=1, source_target_pairs={{0,96},{1,25},{2,98},{3,27},{4,100},{5,29},{6,102},{7,31},{8,104},... | collective-permute-start | bytes 7077896 | tf_op jit(solution)/shard_map/ppermute | solution.py:42
  97.6 22.9 %copy-start.3 = (bf16[4,384,768]{2,1,0:T(8,128)(2,1)}, bf16[4,384,768]{2,1,0:T(8,128)(2,1)S(1)}, u32[]{:S(2)}) copy-start(bf16[4,384,768]{2,1,0:T(8,128)(2,1)S(1)} %collective-permute-done.4.up_ref.w1.refs_1_) | copy-start | bytes 7077892
  129.3 29.2 %collective-permute-start.10 = (bf16[2,768,384]{2,1,0:T(8,128)(2,1)}, bf16[2,768,384]{2,1,0:T(8,128)(2,1)}, u32[]{:S(2)}, u32[]{:S(2)}) collective-permute-start(bf16[2,768,384]{2,1,0:T(8,128)(2,1)} %get-tuple-element.30), channel_id=1, source_target_pairs={{0,32},{1,9},{2,34},{3,11},{4,36},{5,13},{6,38},{7,15},{8,40},{9,1... | collective-permute-start | bytes 3538952 | tf_op jit(solution)/shard_map/ppermute | solution.py:42
  129.3 9.7 %copy-start.4 = (bf16[4,384,768]{2,1,0:T(8,128)(2,1)S(1)}, bf16[4,384,768]{2,1,0:T(8,128)(2,1)}, u32[]{:S(2)}) copy-start(bf16[4,384,768]{2,1,0:T(8,128)(2,1)} %copy-done.3) | copy-start | bytes 7077892
  129.3 29.2 %collective-permute-start.11 = (bf16[2,768,384]{2,1,0:T(8,128)(2,1)}, bf16[2,768,384]{2,1,0:T(8,128)(2,1)}, u32[]{:S(2)}, u32[]{:S(2)}) collective-permute-start(bf16[2,768,384]{2,1,0:T(8,128)(2,1)} %get-tuple-element.31), channel_id=1, source_target_pairs={{0,96},{1,25},{2,98},{3,27},{4,100},{5,29},{6,102},{7,31},{8,104},... | collective-permute-start | bytes 3538952 | tf_op jit(solution)/shard_map/ppermute | solution.py:42
  135.7 33.7 %collective-permute-start.6 = (bf16[2,384,768]{2,1,0:T(8,128)(2,1)}, bf16[2,384,768]{2,1,0:T(8,128)(2,1)S(1)}, u32[]{:S(2)}, u32[]{:S(2)}) collective-permute-start(bf16[2,384,768]{2,1,0:T(8,128)(2,1)} %get-tuple-element.14), channel_id=1, source_target_pairs={{0,8},{1,33},{2,10},{3,35},{4,12},{5,37},{6,14},{7,39},{8,16},{9,4... | collective-permute-start | bytes 3538952 | tf_op jit(solution)/shard_map/ppermute | solution.py:42
  135.7 33.7 %collective-permute-start.7 = (bf16[2,384,768]{2,1,0:T(8,128)(2,1)}, bf16[2,384,768]{2,1,0:T(8,128)(2,1)}, u32[]{:S(2)}, u32[]{:S(2)}) collective-permute-start(bf16[2,384,768]{2,1,0:T(8,128)(2,1)} %get-tuple-element.15), channel_id=1, source_target_pairs={{0,24},{1,97},{2,26},{3,99},{4,28},{5,101},{6,30},{7,103},{8,0},{9... | collective-permute-start | bytes 3538952 | tf_op jit(solution)/shard_map/ppermute | solution.py:42
  156.8 1.7 copy-start.1
  158.5 1.7 copy-start.7
  164.4 0.8 copy-start.15
  164.4 1.0 copy-start.13
  164.4 5.0 %copy-start.2 = (f32[2,1024,384]{2,1,0:T(8,128)S(1)}, f32[2,1024,384]{2,1,0:T(8,128)}, u32[]{:S(2)}) copy-start(f32[2,1024,384]{2,1,0:T(8,128)} %copy-done.1) | copy-start | bytes 9437188
  165.2 12.6 %collective-permute-start.13 = (bf16[2,384,384]{2,1,0:T(8,128)(2,1)S(1)}, bf16[2,384,384]{2,1,0:T(8,128)(2,1)S(1)}, u32[]{:S(2)}, u32[]{:S(2)}) collective-permute-start(bf16[2,384,384]{2,1,0:T(8,128)(2,1)S(1)} %pad_maximum_fusion.2), channel_id=1, source_target_pairs={{0,8},{1,33},{2,10},{3,35},{4,12},{5,37},{6,14},{7,39},{8,16},{9,4... | collective-permute-start | bytes 1769480 | tf_op jit(solution)/shard_map/ppermute | solution.py:42
  166.4 15.2 %collective-permute-start.12 = (bf16[2,384,384]{2,1,0:T(8,128)(2,1)}, bf16[2,384,384]{2,1,0:T(8,128)(2,1)}, u32[]{:S(2)}, u32[]{:S(2)}) collective-permute-start(bf16[2,384,384]{2,1,0:T(8,128)(2,1)} %pad_maximum_fusion.1), channel_id=1, source_target_pairs={{0,24},{1,97},{2,26},{3,99},{4,28},{5,101},{6,30},{7,103},{8,0},{9... | collective-permute-start | bytes 1769480 | tf_op jit(solution)/shard_map/ppermute | solution.py:42
  177.8 0.8 copy-start.21
  178.6 1.1 copy-start.16
  178.6 3.0 %copy-start.14 = (bf16[1,768,384]{2,1,0:T(8,128)(2,1)S(1)}, bf16[1,768,384]{2,1,0:T(8,128)(2,1)}, u32[]{:S(2)}) copy-start(bf16[1,768,384]{2,1,0:T(8,128)(2,1)} %copy-done.13) | copy-start | bytes 1769476
  179.7 6.9 %copy-start.12 = (f32[1024,384]{1,0:T(8,128)S(1)}, f32[1024,384]{1,0:T(8,128)}, u32[]{:S(2)}) copy-start(f32[1024,384]{1,0:T(8,128)} %all-gather.7.cloned.1.call-done) | copy-start | bytes 4718596
  181.6 9.6 %copy-start.20 = (bf16[1,768,384]{2,1,0:T(8,128)(2,1)S(1)}, bf16[1,768,384]{2,1,0:T(8,128)(2,1)}, u32[]{:S(2)}) copy-start(bf16[1,768,384]{2,1,0:T(8,128)(2,1)} %get-tuple-element.24) | copy-start | bytes 1769476
  181.6 9.6 %copy-start.22 = (bf16[2,384,384]{2,1,0:T(8,128)(2,1)S(1)}, bf16[2,384,384]{2,1,0:T(8,128)(2,1)}, u32[]{:S(2)}) copy-start(bf16[2,384,384]{2,1,0:T(8,128)(2,1)} %tie.9) | copy-start | bytes 1769476
  181.6 8.2 %collective-permute-start.14 = (bf16[384,384]{1,0:T(8,128)(2,1)}, bf16[384,384]{1,0:T(8,128)(2,1)}, u32[]{:S(2)}, u32[]{:S(2)}) collective-permute-start(bf16[384,384]{1,0:T(8,128)(2,1)} %fusion.1), channel_id=1, source_target_pairs={{0,8},{1,33},{2,10},{3,35},{4,12},{5,37},{6,14},{7,39},{8,16},{9,4... | collective-permute-start | bytes 884744 | tf_op jit(solution)/shard_map/ppermute | solution.py:42
  183.4 7.7 %collective-permute-start.15 = (bf16[384,384]{1,0:T(8,128)(2,1)}, bf16[384,384]{1,0:T(8,128)(2,1)S(1)}, u32[]{:S(2)}, u32[]{:S(2)}) collective-permute-start(bf16[384,384]{1,0:T(8,128)(2,1)} %fusion.2), channel_id=1, source_target_pairs={{0,24},{1,97},{2,26},{3,99},{4,28},{5,101},{6,30},{7,103},{8,0},{9... | collective-permute-start | bytes 884744 | tf_op jit(solution)/shard_map/ppermute | solution.py:42
Sparse Core Ops, SparseCore 0:
  9.7 72.8 all-gather.4
  85.4 64.7 all-gather.6
